TPU v7x, 512 devices: a whole 4x8x8 slice. The times are simulated.
512 devices in a mesh: blk: 16 (over y, x_lo), shard: 32 (over x_hi, z, core).
Axes of the slice: x: 4 (x_hi: 2, x_lo: 2; x = x_hi * 2 + x_lo), y: 8, z: 8, core: 2. Of those that a mesh axis runs over, the one named last changes fastest.
Arguments:
- queries: float32 [65536, 3584], P(('blk', 'shard')), may hold values from -0.25 to 0.25
- passages: float32 [4096, 3584], P(('blk', 'shard')), may hold values from -0.25 to 0.25
- positive: int32 [65536], P(('blk', 'shard')), may hold values from 0 to 127
- neg_owner: int32 [65536, 7], P(('blk', 'shard')), may hold values from 0 to 31, all different within a row; in each aligned block of 128 rows (0 to 127, 128 to 255, ...) at most 32 rows name the same one
- neg_row: int32 [65536, 7], P(('blk', 'shard')), may hold values from 0 to 7
Outputs:
- query_gradient: float32 [65536, 3584], P(('blk', 'shard'))
- passage_gradient: float32 [4096, 3584], P(('blk', 'shard'))
- losses: float32 [65536], P(('blk', 'shard'))
Inputs may be any that keep to these rules, and one draw needn't show every extreme that they name: `neg_owner`: the 7 owners of one query are distinct; among the rows of one device no shard is named more than 32 times, and in some device's rows one shard is named exactly 32 times.
All inputs are finite; a program needn't handle non-finite values.
Results may differ from a plain program's by a relative error of at most 0.015.
Values may be sent and summed in bfloat16 or wider, within the bound.
A program may use at most 64 MiB of HBM per device.

v0:
```python
import jax
import jax.numpy as jnp
from jax import lax
from jax.sharding import PartitionSpec as P

SOFTMAX_TEMP = 0.05


def passed_along(value, axis, steps):
    count = lax.axis_size(axis)
    pairs = [(source, (source + steps) % count) for source in range(count)]
    return lax.ppermute(value, axis, pairs)


def body(queries, passages, positive, neg_owner, neg_row):
    nblk = lax.axis_size("blk")
    nshard = lax.axis_size("shard")
    myblk = lax.axis_index("blk")
    query_block = queries.astype(jnp.bfloat16)
    pb = passages.astype(jnp.bfloat16)
    rows_q, width = query_block.shape
    rows_p = pb.shape[0]
    negs = neg_owner.shape[1]
    group = nblk * rows_p
    capacity = rows_q * 8 // nshard
    owner = neg_owner.reshape(-1)
    wanted = neg_row.reshape(-1)
    bank_index = owner * rows_p + wanted
    owner_hot = (owner[:, None] == jnp.arange(nshard, dtype=jnp.int32)[None, :]).astype(jnp.int32)
    rank = jnp.sum((jnp.cumsum(owner_hot, 0) - owner_hot) * owner_hot, 1)
    slot = owner * capacity + rank
    requests = (
        jnp.full((nshard * capacity,), rows_p, jnp.int32)
        .at[slot]
        .set(wanted)
        .reshape(nshard, capacity)
    )
    incoming = lax.all_to_all(requests, "shard", split_axis=0, concat_axis=0, tiled=True)
    padded = jnp.concatenate([pb, jnp.zeros((1, width), jnp.bfloat16)], 0)
    served = padded[incoming]
    fetched = lax.all_to_all(served, "shard", split_axis=0, concat_axis=0, tiled=True)
    order_index = slot.reshape(rows_q, negs).T.reshape(-1)
    hard_negative_rows = fetched.reshape(-1, width)[order_index]
    hard_negative_rows = hard_negative_rows.reshape(negs, rows_q, width)
    hardneg_scores = (
        jnp.einsum(
            "qd,kqd->kq", query_block, hard_negative_rows, preferred_element_type=jnp.float32
        ).T
        / SOFTMAX_TEMP
    )
    passage_store = jnp.zeros((nblk, rows_p, width), jnp.bfloat16)
    passage_store = lax.dynamic_update_slice(passage_store, pb[None], (myblk, 0, 0))

    def visit(step, carry):
        block, kept = carry
        block = passed_along(block, "blk", 1)
        anchor = (myblk - step) % nblk
        kept = lax.dynamic_update_slice(kept, block[None], (anchor, 0, 0))
        return (block, kept)

    unused, passage_store = lax.fori_loop(1, nblk, visit, (pb, passage_store))
    passage_store = passage_store.reshape(group, width)
    inbatch_scores = (
        jnp.einsum("bm,lm->bl", query_block, passage_store, preferred_element_type=jnp.float32)
        / SOFTMAX_TEMP
    )
    top = jnp.maximum(jnp.max(inbatch_scores, -1), jnp.max(hardneg_scores, -1))
    total = jnp.sum(jnp.exp(inbatch_scores - top[:, None]), -1) + jnp.sum(
        jnp.exp(hardneg_scores - top[:, None]), -1
    )
    lse = top + jnp.log(total)
    hit = jnp.arange(group, dtype=jnp.int32)[None, :] == positive[:, None]
    chosen = jnp.sum(jnp.where(hit, inbatch_scores, jnp.float32(0.0)), -1)
    losses = lse - chosen
    w_in = (jnp.exp(inbatch_scores - lse[:, None]) - hit.astype(jnp.float32)).astype(jnp.bfloat16)
    w_hn = jnp.exp(hardneg_scores - lse[:, None]).astype(jnp.bfloat16)
    inbatch_gradient = jnp.einsum(
        "qp,pd->qd", w_in, passage_store, preferred_element_type=jnp.float32
    )
    hardneg_gradient = jnp.einsum(
        "kq,kqd->qd", w_hn.T, hard_negative_rows, preferred_element_type=jnp.float32
    )
    query_gradient = (inbatch_gradient + hardneg_gradient) / SOFTMAX_TEMP
    columns = jnp.arange(nshard * rows_p, dtype=jnp.int32)
    selector = (bank_index[:, None] == columns[None, :]).astype(jnp.bfloat16) * w_hn.reshape(-1)[
        :, None
    ]
    selector = jnp.sum(selector.reshape(rows_q, negs, nshard * rows_p), 1)
    part = (
        jnp.einsum("qc,qd->cd", selector, query_block, preferred_element_type=jnp.float32)
        / SOFTMAX_TEMP
    ).astype(jnp.bfloat16)
    returned = lax.all_to_all(
        part.reshape(nshard, rows_p, width), "shard", split_axis=0, concat_axis=0, tiled=True
    )
    hard_grad = jnp.sum(returned.astype(jnp.float32), 0)

    def block_term(start, count):
        column_indices = lax.dynamic_slice_in_dim(w_in, start, count, 1)
        return (
            jnp.einsum("ok,oe->ke", column_indices, query_block, preferred_element_type=jnp.float32)
            / SOFTMAX_TEMP
        )

    carried = block_term((myblk - 1) % nblk * rows_p, rows_p)

    def pass_on(step, acc):
        acc = passed_along(acc.astype(jnp.bfloat16), "blk", 1).astype(acc.dtype)
        return acc + block_term((myblk - 1 - step) % nblk * rows_p, rows_p)

    carried = lax.fori_loop(1, nblk, pass_on, carried)
    passage_gradient = carried + hard_grad
    return (query_gradient, passage_gradient, losses)


def solution(mesh):
    in_specs = (
        P(("blk", "shard"), None),
        P(("blk", "shard"), None),
        P(("blk", "shard")),
        P(("blk", "shard"), None),
        P(("blk", "shard"), None),
    )
    out_specs = (P(("blk", "shard"), None), P(("blk", "shard"), None), P(("blk", "shard")))
    return jax.shard_map(body, mesh=mesh, in_specs=in_specs, out_specs=out_specs, check_vma=False)
```

profile of v0, /device:TPU:64, one launch (start us, length us, event | category | flops | bytes accessed | tf_op | source)
XLA Modules:
  0.0 427.3 jit_solution(18275378846991445501)
XLA Ops:
  5.8 5.3 %scatter_custom_fusion = s32[1024]{0:T(1024)S(1)} fusion(s32[896]{0:T(1024)S(1)} %fusion.25, s32[896]{0:T(1024)S(1)} %reshape.199, s32[]{:T(128)} %constant.170.clone.1), kind=kCustom, calls=%fused_computation.61 | custom fusion | bytes 4100 | tf_op jit(solution)/shard_map/scatter | solution.py:35
  11.8 12.6 %all-to-all-start = ((s32[32,1,32]{2,1,0:T(1,128)}), s32[32,1,32]{2,1,0:T(1,128)S(1)}, u32[]{:S(2)}, u32[]{:S(2)}) async-start(s32[32,1,32]{2,1,0:T(1,128)} %all_to_all.14), calls=%async_computation | async-start | bytes 32768 | tf_op jit(solution)/shard_map/all_to_all | solution.py:38
  27.8 5.2 %all-to-all-done = s32[32,1,32]{2,1,0:T(1,128)S(1)} async-done(((s32[32,1,32]{2,1,0:T(1,128)}), s32[32,1,32]{2,1,0:T(1,128)S(1)}, u32[]{:S(2)}, u32[]{:S(2)}) %all-to-all-start) | async-done | bytes 4128 | tf_op jit(solution)/shard_map/all_to_all | solution.py:38
  33.1 7.3 %gather_fusion = bf16[1024,3584]{1,0:T(8,128)(2,1)} fusion(bf16[9,3584]{1,0:T(8,128)(2,1)S(1)} %concatenate.3, s32[1024]{0:T(1024)S(1)} %broadcast_clamp_fusion), kind=kCustom, calls=%fused_computation | custom fusion | bytes 14684160 | tf_op jit(solution)/shard_map/gather | solution.py:40
  40.4 5.9 %all-to-all-start.1 = ((bf16[32,32,3584]{2,1,0:T(8,128)(2,1)}), bf16[32,32,3584]{2,1,0:T(8,128)(2,1)}, u32[]{:S(2)}, u32[]{:S(2)}) async-start(bf16[32,32,3584]{2,1,0:T(8,128)(2,1)} %bitcast.93), calls=%async_computation.1 | async-start | bytes 14680064 | tf_op jit(solution)/shard_map/all_to_all | solution.py:41
  46.4 141.6 %while.32 = (s32[]{:T(128)}, bf16[8,3584]{1,0:T(8,128)(2,1)S(1)}, bf16[16,8,3584]{2,1,0:T(8,128)(2,1)S(1)}, s32[]{:T(128)}, s32[]{:T(128)}, /*index=5*/s32[]{:T(128)}, s32[]{:T(128)}, s32[]{:T(128)}) while((s32[]{:T(128)}, bf16[8,3584]{1,0:T(8,128)(2,1)S(1)}, bf16[16,8,3584]{2,1,0:T(8,128)(2,1)S(1)}, s32[]{:T(128)}, s32[]{:T(128)}, ...), condition=%wide.region_1.2_spmd, body=%wide.region_0.0_spmd.sunk | while | flops 17 | bytes 459036 | solution.py:61
  48.9 10.9 %collective-permute-done = bf16[8,3584]{1,0:T(8,128)(2,1)S(1)} collective-permute-done((bf16[8,3584]{1,0:T(8,128)(2,1)S(1)}, bf16[8,3584]{1,0:T(8,128)(2,1)S(1)}, u32[]{:S(2)}, u32[]{:S(2)}) %collective-permute-start) | collective-permute-done | bytes 57376 | tf_op jit(solution)/shard_map/while/body/eval_jaxpr/ppermute | solution.py:12
  59.8 4.5 %collective-permute-start = (bf16[8,3584]{1,0:T(8,128)(2,1)S(1)}, bf16[8,3584]{1,0:T(8,128)(2,1)S(1)}, u32[]{:S(2)}, u32[]{:S(2)}) collective-permute-start(bf16[8,3584]{1,0:T(8,128)(2,1)S(1)} %get-tuple-element.360), channel_id=1, source_target_pairs={{0,32},{32,64},{64,96},{96,128},{128,160},{160,192},{192,224},{224... | collective-permute-start | bytes 172040 | tf_op jit(solution)/shard_map/while/body/eval_jaxpr/ppermute | solution.py:12
  64.3 5.5 %collective-permute-done = bf16[8,3584]{1,0:T(8,128)(2,1)S(1)} collective-permute-done((bf16[8,3584]{1,0:T(8,128)(2,1)S(1)}, bf16[8,3584]{1,0:T(8,128)(2,1)S(1)}, u32[]{:S(2)}, u32[]{:S(2)}) %collective-permute-start) | collective-permute-done | bytes 57376 | tf_op jit(solution)/shard_map/while/body/eval_jaxpr/ppermute | solution.py:12
  69.8 3.4 collective-permute-start
  73.2 6.6 %collective-permute-done = bf16[8,3584]{1,0:T(8,128)(2,1)S(1)} collective-permute-done((bf16[8,3584]{1,0:T(8,128)(2,1)S(1)}, bf16[8,3584]{1,0:T(8,128)(2,1)S(1)}, u32[]{:S(2)}, u32[]{:S(2)}) %collective-permute-start) | collective-permute-done | bytes 57376 | tf_op jit(solution)/shard_map/while/body/eval_jaxpr/ppermute | solution.py:12
  83.3 5.0 %collective-permute-done = bf16[8,3584]{1,0:T(8,128)(2,1)S(1)} collective-permute-done((bf16[8,3584]{1,0:T(8,128)(2,1)S(1)}, bf16[8,3584]{1,0:T(8,128)(2,1)S(1)}, u32[]{:S(2)}, u32[]{:S(2)}) %collective-permute-start) | collective-permute-done | bytes 57376 | tf_op jit(solution)/shard_map/while/body/eval_jaxpr/ppermute | solution.py:12
  90.3 6.4 %collective-permute-done = bf16[8,3584]{1,0:T(8,128)(2,1)S(1)} collective-permute-done((bf16[8,3584]{1,0:T(8,128)(2,1)S(1)}, bf16[8,3584]{1,0:T(8,128)(2,1)S(1)}, u32[]{:S(2)}, u32[]{:S(2)}) %collective-permute-start) | collective-permute-done | bytes 57376 | tf_op jit(solution)/shard_map/while/body/eval_jaxpr/ppermute | solution.py:12
  98.7 6.8 %collective-permute-done = bf16[8,3584]{1,0:T(8,128)(2,1)S(1)} collective-permute-done((bf16[8,3584]{1,0:T(8,128)(2,1)S(1)}, bf16[8,3584]{1,0:T(8,128)(2,1)S(1)}, u32[]{:S(2)}, u32[]{:S(2)}) %collective-permute-start) | collective-permute-done | bytes 57376 | tf_op jit(solution)/shard_map/while/body/eval_jaxpr/ppermute | solution.py:12
  107.4 6.5 %collective-permute-done = bf16[8,3584]{1,0:T(8,128)(2,1)S(1)} collective-permute-done((bf16[8,3584]{1,0:T(8,128)(2,1)S(1)}, bf16[8,3584]{1,0:T(8,128)(2,1)S(1)}, u32[]{:S(2)}, u32[]{:S(2)}) %collective-permute-start) | collective-permute-done | bytes 57376 | tf_op jit(solution)/shard_map/while/body/eval_jaxpr/ppermute | solution.py:12
  115.9 7.2 %collective-permute-done = bf16[8,3584]{1,0:T(8,128)(2,1)S(1)} collective-permute-done((bf16[8,3584]{1,0:T(8,128)(2,1)S(1)}, bf16[8,3584]{1,0:T(8,128)(2,1)S(1)}, u32[]{:S(2)}, u32[]{:S(2)}) %collective-permute-start) | collective-permute-done | bytes 57376 | tf_op jit(solution)/shard_map/while/body/eval_jaxpr/ppermute | solution.py:12
  123.2 3.4 collective-permute-start
  126.7 6.2 %collective-permute-done = bf16[8,3584]{1,0:T(8,128)(2,1)S(1)} collective-permute-done((bf16[8,3584]{1,0:T(8,128)(2,1)S(1)}, bf16[8,3584]{1,0:T(8,128)(2,1)S(1)}, u32[]{:S(2)}, u32[]{:S(2)}) %collective-permute-start) | collective-permute-done | bytes 57376 | tf_op jit(solution)/shard_map/while/body/eval_jaxpr/ppermute | solution.py:12
  134.8 6.2 %collective-permute-done = bf16[8,3584]{1,0:T(8,128)(2,1)S(1)} collective-permute-done((bf16[8,3584]{1,0:T(8,128)(2,1)S(1)}, bf16[8,3584]{1,0:T(8,128)(2,1)S(1)}, u32[]{:S(2)}, u32[]{:S(2)}) %collective-permute-start) | collective-permute-done | bytes 57376 | tf_op jit(solution)/shard_map/while/body/eval_jaxpr/ppermute | solution.py:12
  143.0 6.2 %collective-permute-done = bf16[8,3584]{1,0:T(8,128)(2,1)S(1)} collective-permute-done((bf16[8,3584]{1,0:T(8,128)(2,1)S(1)}, bf16[8,3584]{1,0:T(8,128)(2,1)S(1)}, u32[]{:S(2)}, u32[]{:S(2)}) %collective-permute-start) | collective-permute-done | bytes 57376 | tf_op jit(solution)/shard_map/while/body/eval_jaxpr/ppermute | solution.py:12
  151.2 6.2 %collective-permute-done = bf16[8,3584]{1,0:T(8,128)(2,1)S(1)} collective-permute-done((bf16[8,3584]{1,0:T(8,128)(2,1)S(1)}, bf16[8,3584]{1,0:T(8,128)(2,1)S(1)}, u32[]{:S(2)}, u32[]{:S(2)}) %collective-permute-start) | collective-permute-done | bytes 57376 | tf_op jit(solution)/shard_map/while/body/eval_jaxpr/ppermute | solution.py:12
  159.5 6.7 %collective-permute-done = bf16[8,3584]{1,0:T(8,128)(2,1)S(1)} collective-permute-done((bf16[8,3584]{1,0:T(8,128)(2,1)S(1)}, bf16[8,3584]{1,0:T(8,128)(2,1)S(1)}, u32[]{:S(2)}, u32[]{:S(2)}) %collective-permute-start) | collective-permute-done | bytes 57376 | tf_op jit(solution)/shard_map/while/body/eval_jaxpr/ppermute | solution.py:12
  168.1 11.0 %collective-permute-done = bf16[8,3584]{1,0:T(8,128)(2,1)S(1)} collective-permute-done((bf16[8,3584]{1,0:T(8,128)(2,1)S(1)}, bf16[8,3584]{1,0:T(8,128)(2,1)S(1)}, u32[]{:S(2)}, u32[]{:S(2)}) %collective-permute-start) | collective-permute-done | bytes 57376 | tf_op jit(solution)/shard_map/while/body/eval_jaxpr/ppermute | solution.py:12
  179.2 4.8 %collective-permute-start = (bf16[8,3584]{1,0:T(8,128)(2,1)S(1)}, bf16[8,3584]{1,0:T(8,128)(2,1)S(1)}, u32[]{:S(2)}, u32[]{:S(2)}) collective-permute-start(bf16[8,3584]{1,0:T(8,128)(2,1)S(1)} %get-tuple-element.360), channel_id=1, source_target_pairs={{0,32},{32,64},{64,96},{96,128},{128,160},{160,192},{192,224},{224... | collective-permute-start | bytes 172040 | tf_op jit(solution)/shard_map/while/body/eval_jaxpr/ppermute | solution.py:12
  184.0 3.9 collective-permute-done
  189.9 18.8 %all-to-all-done.1 = bf16[32,32,3584]{2,1,0:T(8,128)(2,1)} async-done(((bf16[32,32,3584]{2,1,0:T(8,128)(2,1)}), bf16[32,32,3584]{2,1,0:T(8,128)(2,1)}, u32[]{:S(2)}, u32[]{:S(2)}) %all-to-all-start.1) | async-done | bytes 7340064 | tf_op jit(solution)/shard_map/all_to_all | solution.py:41
  208.7 17.8 %gather_fusion.1 = bf16[896,3584]{1,0:T(8,128)(2,1)} fusion(bf16[1024,3584]{1,0:T(8,128)(2,1)} %bitcast.7, s32[1024]{0:T(1024)S(1)} %pad_clamp_fusion), kind=kCustom, calls=%fused_computation.1 | custom fusion | bytes 12848640 | tf_op jit(solution)/shard_map/gather | solution.py:43
  226.6 7.9 %fusion.4 = f32[128,1,7]{2,1,0:T(1,128)S(1)} fusion(bf16[7,128,3584]{2,1,0:T(8,128)(2,1)} %bitcast.91, bf16[128,3584,1]{1,0,2:T(8,128)(2,1)S(1)} %convert_bitcast_fusion), kind=kOutput, calls=%fused_computation.10 | convolution fusion | flops 6422528 | bytes 7343616 | tf_op jit(solution)/shard_map/qd,kqd->kq/dot_general | solution.py:46
  237.4 10.6 %all-to-all-start.2 = ((bf16[32,8,3584]{2,1,0:T(8,128)(2,1)}), bf16[32,8,3584]{2,1,0:T(8,128)(2,1)}, u32[]{:S(2)}, u32[]{:S(2)}) async-start(bf16[32,8,3584]{2,1,0:T(8,128)(2,1)} %fusion.8), calls=%async_computation.2 | async-start | bytes 3670016 | tf_op jit(solution)/shard_map/all_to_all | solution.py:93
  248.4 7.8 %fusion.2 = f32[128,1,3584]{2,1,0:T(1,128)S(1)} fusion(bf16[7,128,1]{0,2,1:T(2,128)(2,1)S(1)} %copy.28, bf16[7,128,3584]{2,1,0:T(8,128)(2,1)} %bitcast.92), kind=kOutput, calls=%fused_computation.8 | convolution fusion | flops 6422528 | bytes 8259328 | tf_op jit(solution)/shard_map/kq,kqd->qd/dot_general | solution.py:80
  257.9 37.5 %all-to-all-done.2 = bf16[32,8,3584]{2,1,0:T(8,128)(2,1)} async-done(((bf16[32,8,3584]{2,1,0:T(8,128)(2,1)}), bf16[32,8,3584]{2,1,0:T(8,128)(2,1)}, u32[]{:S(2)}, u32[]{:S(2)}) %all-to-all-start.2) | async-done | bytes 1835040 | tf_op jit(solution)/shard_map/all_to_all | solution.py:93
  297.1 129.4 %while.33 = (s32[]{:T(128)}, f32[8,3584]{1,0:T(8,128)S(1)}, s32[]{:T(128)}, bf16[128,128]{0,1:T(8,128)(2,1)S(1)}, bf16[128,3584]{1,0:T(8,128)(2,1)S(1)}, /*index...) while((s32[]{:T(128)}, f32[8,3584]{1,0:T(8,128)S(1)}, s32[]{:T(128)}, ...), condition=%wide.region_11.12_spmd, body=%wide.region_10.11_spmd.sunk | while | flops 7454738 | bytes 1493312 | solution.py:111
  297.2 8.9 %collective-permute-start.1 = (bf16[8,3584]{1,0:T(8,128)(2,1)S(1)}, bf16[8,3584]{1,0:T(8,128)(2,1)S(1)}, u32[]{:S(2)}, u32[]{:S(2)}) collective-permute-start(bf16[8,3584]{1,0:T(8,128)(2,1)S(1)} %convert_element_type.82), channel_id=1, source_target_pairs={{0,32},{32,64},{64,96},{96,128},{128,160},{160,192},{192,224},{224... | collective-permute-start | bytes 172040 | tf_op jit(solution)/shard_map/while/body/eval_jaxpr/ppermute | solution.py:12
  308.1 4.3 collective-permute-start.1
  312.4 3.9 collective-permute-done.1
  318.8 6.0 %collective-permute-done.1 = bf16[8,3584]{1,0:T(8,128)(2,1)S(1)} collective-permute-done((bf16[8,3584]{1,0:T(8,128)(2,1)S(1)}, bf16[8,3584]{1,0:T(8,128)(2,1)S(1)}, u32[]{:S(2)}, u32[]{:S(2)}) %collective-permute-start.1) | collective-permute-done | bytes 57376 | tf_op jit(solution)/shard_map/while/body/eval_jaxpr/ppermute | solution.py:12
  327.0 6.2 %collective-permute-done.1 = bf16[8,3584]{1,0:T(8,128)(2,1)S(1)} collective-permute-done((bf16[8,3584]{1,0:T(8,128)(2,1)S(1)}, bf16[8,3584]{1,0:T(8,128)(2,1)S(1)}, u32[]{:S(2)}, u32[]{:S(2)}) %collective-permute-start.1) | collective-permute-done | bytes 57376 | tf_op jit(solution)/shard_map/while/body/eval_jaxpr/ppermute | solution.py:12
  335.4 6.2 %collective-permute-done.1 = bf16[8,3584]{1,0:T(8,128)(2,1)S(1)} collective-permute-done((bf16[8,3584]{1,0:T(8,128)(2,1)S(1)}, bf16[8,3584]{1,0:T(8,128)(2,1)S(1)}, u32[]{:S(2)}, u32[]{:S(2)}) %collective-permute-start.1) | collective-permute-done | bytes 57376 | tf_op jit(solution)/shard_map/while/body/eval_jaxpr/ppermute | solution.py:12
  343.8 6.4 %collective-permute-done.1 = bf16[8,3584]{1,0:T(8,128)(2,1)S(1)} collective-permute-done((bf16[8,3584]{1,0:T(8,128)(2,1)S(1)}, bf16[8,3584]{1,0:T(8,128)(2,1)S(1)}, u32[]{:S(2)}, u32[]{:S(2)}) %collective-permute-start.1) | collective-permute-done | bytes 57376 | tf_op jit(solution)/shard_map/while/body/eval_jaxpr/ppermute | solution.py:12
  352.4 6.2 %collective-permute-done.1 = bf16[8,3584]{1,0:T(8,128)(2,1)S(1)} collective-permute-done((bf16[8,3584]{1,0:T(8,128)(2,1)S(1)}, bf16[8,3584]{1,0:T(8,128)(2,1)S(1)}, u32[]{:S(2)}, u32[]{:S(2)}) %collective-permute-start.1) | collective-permute-done | bytes 57376 | tf_op jit(solution)/shard_map/while/body/eval_jaxpr/ppermute | solution.py:12
  360.9 6.2 %collective-permute-done.1 = bf16[8,3584]{1,0:T(8,128)(2,1)S(1)} collective-permute-done((bf16[8,3584]{1,0:T(8,128)(2,1)S(1)}, bf16[8,3584]{1,0:T(8,128)(2,1)S(1)}, u32[]{:S(2)}, u32[]{:S(2)}) %collective-permute-start.1) | collective-permute-done | bytes 57376 | tf_op jit(solution)/shard_map/while/body/eval_jaxpr/ppermute | solution.py:12
  369.3 6.2 %collective-permute-done.1 = bf16[8,3584]{1,0:T(8,128)(2,1)S(1)} collective-permute-done((bf16[8,3584]{1,0:T(8,128)(2,1)S(1)}, bf16[8,3584]{1,0:T(8,128)(2,1)S(1)}, u32[]{:S(2)}, u32[]{:S(2)}) %collective-permute-start.1) | collective-permute-done | bytes 57376 | tf_op jit(solution)/shard_map/while/body/eval_jaxpr/ppermute | solution.py:12
  377.7 6.2 %collective-permute-done.1 = bf16[8,3584]{1,0:T(8,128)(2,1)S(1)} collective-permute-done((bf16[8,3584]{1,0:T(8,128)(2,1)S(1)}, bf16[8,3584]{1,0:T(8,128)(2,1)S(1)}, u32[]{:S(2)}, u32[]{:S(2)}) %collective-permute-start.1) | collective-permute-done | bytes 57376 | tf_op jit(solution)/shard_map/while/body/eval_jaxpr/ppermute | solution.py:12
  386.1 6.2 %collective-permute-done.1 = bf16[8,3584]{1,0:T(8,128)(2,1)S(1)} collective-permute-done((bf16[8,3584]{1,0:T(8,128)(2,1)S(1)}, bf16[8,3584]{1,0:T(8,128)(2,1)S(1)}, u32[]{:S(2)}, u32[]{:S(2)}) %collective-permute-start.1) | collective-permute-done | bytes 57376 | tf_op jit(solution)/shard_map/while/body/eval_jaxpr/ppermute | solution.py:12
  394.6 6.2 %collective-permute-done.1 = bf16[8,3584]{1,0:T(8,128)(2,1)S(1)} collective-permute-done((bf16[8,3584]{1,0:T(8,128)(2,1)S(1)}, bf16[8,3584]{1,0:T(8,128)(2,1)S(1)}, u32[]{:S(2)}, u32[]{:S(2)}) %collective-permute-start.1) | collective-permute-done | bytes 57376 | tf_op jit(solution)/shard_map/while/body/eval_jaxpr/ppermute | solution.py:12
  403.0 6.5 %collective-permute-done.1 = bf16[8,3584]{1,0:T(8,128)(2,1)S(1)} collective-permute-done((bf16[8,3584]{1,0:T(8,128)(2,1)S(1)}, bf16[8,3584]{1,0:T(8,128)(2,1)S(1)}, u32[]{:S(2)}, u32[]{:S(2)}) %collective-permute-start.1) | collective-permute-done | bytes 57376 | tf_op jit(solution)/shard_map/while/body/eval_jaxpr/ppermute | solution.py:12
  411.7 6.2 %collective-permute-done.1 = bf16[8,3584]{1,0:T(8,128)(2,1)S(1)} collective-permute-done((bf16[8,3584]{1,0:T(8,128)(2,1)S(1)}, bf16[8,3584]{1,0:T(8,128)(2,1)S(1)}, u32[]{:S(2)}, u32[]{:S(2)}) %collective-permute-start.1) | collective-permute-done | bytes 57376 | tf_op jit(solution)/shard_map/while/body/eval_jaxpr/ppermute | solution.py:12
  420.1 6.2 %collective-permute-done.1 = bf16[8,3584]{1,0:T(8,128)(2,1)S(1)} collective-permute-done((bf16[8,3584]{1,0:T(8,128)(2,1)S(1)}, bf16[8,3584]{1,0:T(8,128)(2,1)S(1)}, u32[]{:S(2)}, u32[]{:S(2)}) %collective-permute-start.1) | collective-permute-done | bytes 57376 | tf_op jit(solution)/shard_map/while/body/eval_jaxpr/ppermute | solution.py:12
  (131 shorter events, 72.5 us)
Async XLA Ops:
  11.8 21.2 %all-to-all-start = ((s32[32,1,32]{2,1,0:T(1,128)}), s32[32,1,32]{2,1,0:T(1,128)S(1)}, u32[]{:S(2)}, u32[]{:S(2)}) async-start(s32[32,1,32]{2,1,0:T(1,128)} %all_to_all.14), calls=%async_computation | async-start | bytes 32768 | tf_op jit(solution)/shard_map/all_to_all | solution.py:38
  40.4 168.3 %all-to-all-start.1 = ((bf16[32,32,3584]{2,1,0:T(8,128)(2,1)}), bf16[32,32,3584]{2,1,0:T(8,128)(2,1)}, u32[]{:S(2)}, u32[]{:S(2)}) async-start(bf16[32,32,3584]{2,1,0:T(8,128)(2,1)} %bitcast.93), calls=%async_computation.1 | async-start | bytes 14680064 | tf_op jit(solution)/shard_map/all_to_all | solution.py:41
  46.4 13.4 %collective-permute-start = (bf16[8,3584]{1,0:T(8,128)(2,1)S(1)}, bf16[8,3584]{1,0:T(8,128)(2,1)S(1)}, u32[]{:S(2)}, u32[]{:S(2)}) collective-permute-start(bf16[8,3584]{1,0:T(8,128)(2,1)S(1)} %get-tuple-element.360), channel_id=1, source_target_pairs={{0,32},{32,64},{64,96},{96,128},{128,160},{160,192},{192,224},{224... | collective-permute-start | bytes 172040 | tf_op jit(solution)/shard_map/while/body/eval_jaxpr/ppermute | solution.py:12
  59.8 10.0 %collective-permute-start = (bf16[8,3584]{1,0:T(8,128)(2,1)S(1)}, bf16[8,3584]{1,0:T(8,128)(2,1)S(1)}, u32[]{:S(2)}, u32[]{:S(2)}) collective-permute-start(bf16[8,3584]{1,0:T(8,128)(2,1)S(1)} %get-tuple-element.360), channel_id=1, source_target_pairs={{0,32},{32,64},{64,96},{96,128},{128,160},{160,192},{192,224},{224... | collective-permute-start | bytes 172040 | tf_op jit(solution)/shard_map/while/body/eval_jaxpr/ppermute | solution.py:12
  69.8 10.1 %collective-permute-start = (bf16[8,3584]{1,0:T(8,128)(2,1)S(1)}, bf16[8,3584]{1,0:T(8,128)(2,1)S(1)}, u32[]{:S(2)}, u32[]{:S(2)}) collective-permute-start(bf16[8,3584]{1,0:T(8,128)(2,1)S(1)} %get-tuple-element.360), channel_id=1, source_target_pairs={{0,32},{32,64},{64,96},{96,128},{128,160},{160,192},{192,224},{224... | collective-permute-start | bytes 172040 | tf_op jit(solution)/shard_map/while/body/eval_jaxpr/ppermute | solution.py:12
  79.9 8.4 %collective-permute-start = (bf16[8,3584]{1,0:T(8,128)(2,1)S(1)}, bf16[8,3584]{1,0:T(8,128)(2,1)S(1)}, u32[]{:S(2)}, u32[]{:S(2)}) collective-permute-start(bf16[8,3584]{1,0:T(8,128)(2,1)S(1)} %get-tuple-element.360), channel_id=1, source_target_pairs={{0,32},{32,64},{64,96},{96,128},{128,160},{160,192},{192,224},{224... | collective-permute-start | bytes 172040 | tf_op jit(solution)/shard_map/while/body/eval_jaxpr/ppermute | solution.py:12
  88.3 8.4 %collective-permute-start = (bf16[8,3584]{1,0:T(8,128)(2,1)S(1)}, bf16[8,3584]{1,0:T(8,128)(2,1)S(1)}, u32[]{:S(2)}, u32[]{:S(2)}) collective-permute-start(bf16[8,3584]{1,0:T(8,128)(2,1)S(1)} %get-tuple-element.360), channel_id=1, source_target_pairs={{0,32},{32,64},{64,96},{96,128},{128,160},{160,192},{192,224},{224... | collective-permute-start | bytes 172040 | tf_op jit(solution)/shard_map/while/body/eval_jaxpr/ppermute | solution.py:12
  96.7 8.7 %collective-permute-start = (bf16[8,3584]{1,0:T(8,128)(2,1)S(1)}, bf16[8,3584]{1,0:T(8,128)(2,1)S(1)}, u32[]{:S(2)}, u32[]{:S(2)}) collective-permute-start(bf16[8,3584]{1,0:T(8,128)(2,1)S(1)} %get-tuple-element.360), channel_id=1, source_target_pairs={{0,32},{32,64},{64,96},{96,128},{128,160},{160,192},{192,224},{224... | collective-permute-start | bytes 172040 | tf_op jit(solution)/shard_map/while/body/eval_jaxpr/ppermute | solution.py:12
  105.5 8.5 %collective-permute-start = (bf16[8,3584]{1,0:T(8,128)(2,1)S(1)}, bf16[8,3584]{1,0:T(8,128)(2,1)S(1)}, u32[]{:S(2)}, u32[]{:S(2)}) collective-permute-start(bf16[8,3584]{1,0:T(8,128)(2,1)S(1)} %get-tuple-element.360), channel_id=1, source_target_pairs={{0,32},{32,64},{64,96},{96,128},{128,160},{160,192},{192,224},{224... | collective-permute-start | bytes 172040 | tf_op jit(solution)/shard_map/while/body/eval_jaxpr/ppermute | solution.py:12
  114.0 9.2 %collective-permute-start = (bf16[8,3584]{1,0:T(8,128)(2,1)S(1)}, bf16[8,3584]{1,0:T(8,128)(2,1)S(1)}, u32[]{:S(2)}, u32[]{:S(2)}) collective-permute-start(bf16[8,3584]{1,0:T(8,128)(2,1)S(1)} %get-tuple-element.360), channel_id=1, source_target_pairs={{0,32},{32,64},{64,96},{96,128},{128,160},{160,192},{192,224},{224... | collective-permute-start | bytes 172040 | tf_op jit(solution)/shard_map/while/body/eval_jaxpr/ppermute | solution.py:12
  123.2 9.7 %collective-permute-start = (bf16[8,3584]{1,0:T(8,128)(2,1)S(1)}, bf16[8,3584]{1,0:T(8,128)(2,1)S(1)}, u32[]{:S(2)}, u32[]{:S(2)}) collective-permute-start(bf16[8,3584]{1,0:T(8,128)(2,1)S(1)} %get-tuple-element.360), channel_id=1, source_target_pairs={{0,32},{32,64},{64,96},{96,128},{128,160},{160,192},{192,224},{224... | collective-permute-start | bytes 172040 | tf_op jit(solution)/shard_map/while/body/eval_jaxpr/ppermute | solution.py:12
  132.9 8.2 %collective-permute-start = (bf16[8,3584]{1,0:T(8,128)(2,1)S(1)}, bf16[8,3584]{1,0:T(8,128)(2,1)S(1)}, u32[]{:S(2)}, u32[]{:S(2)}) collective-permute-start(bf16[8,3584]{1,0:T(8,128)(2,1)S(1)} %get-tuple-element.360), channel_id=1, source_target_pairs={{0,32},{32,64},{64,96},{96,128},{128,160},{160,192},{192,224},{224... | collective-permute-start | bytes 172040 | tf_op jit(solution)/shard_map/while/body/eval_jaxpr/ppermute | solution.py:12
  141.1 8.2 %collective-permute-start = (bf16[8,3584]{1,0:T(8,128)(2,1)S(1)}, bf16[8,3584]{1,0:T(8,128)(2,1)S(1)}, u32[]{:S(2)}, u32[]{:S(2)}) collective-permute-start(bf16[8,3584]{1,0:T(8,128)(2,1)S(1)} %get-tuple-element.360), channel_id=1, source_target_pairs={{0,32},{32,64},{64,96},{96,128},{128,160},{160,192},{192,224},{224... | collective-permute-start | bytes 172040 | tf_op jit(solution)/shard_map/while/body/eval_jaxpr/ppermute | solution.py:12
  149.3 8.2 %collective-permute-start = (bf16[8,3584]{1,0:T(8,128)(2,1)S(1)}, bf16[8,3584]{1,0:T(8,128)(2,1)S(1)}, u32[]{:S(2)}, u32[]{:S(2)}) collective-permute-start(bf16[8,3584]{1,0:T(8,128)(2,1)S(1)} %get-tuple-element.360), channel_id=1, source_target_pairs={{0,32},{32,64},{64,96},{96,128},{128,160},{160,192},{192,224},{224... | collective-permute-start | bytes 172040 | tf_op jit(solution)/shard_map/while/body/eval_jaxpr/ppermute | solution.py:12
  157.5 8.6 %collective-permute-start = (bf16[8,3584]{1,0:T(8,128)(2,1)S(1)}, bf16[8,3584]{1,0:T(8,128)(2,1)S(1)}, u32[]{:S(2)}, u32[]{:S(2)}) collective-permute-start(bf16[8,3584]{1,0:T(8,128)(2,1)S(1)} %get-tuple-element.360), channel_id=1, source_target_pairs={{0,32},{32,64},{64,96},{96,128},{128,160},{160,192},{192,224},{224... | collective-permute-start | bytes 172040 | tf_op jit(solution)/shard_map/while/body/eval_jaxpr/ppermute | solution.py:12
  166.2 13.0 %collective-permute-start = (bf16[8,3584]{1,0:T(8,128)(2,1)S(1)}, bf16[8,3584]{1,0:T(8,128)(2,1)S(1)}, u32[]{:S(2)}, u32[]{:S(2)}) collective-permute-start(bf16[8,3584]{1,0:T(8,128)(2,1)S(1)} %get-tuple-element.360), channel_id=1, source_target_pairs={{0,32},{32,64},{64,96},{96,128},{128,160},{160,192},{192,224},{224... | collective-permute-start | bytes 172040 | tf_op jit(solution)/shard_map/while/body/eval_jaxpr/ppermute | solution.py:12
  179.2 8.7 %collective-permute-start = (bf16[8,3584]{1,0:T(8,128)(2,1)S(1)}, bf16[8,3584]{1,0:T(8,128)(2,1)S(1)}, u32[]{:S(2)}, u32[]{:S(2)}) collective-permute-start(bf16[8,3584]{1,0:T(8,128)(2,1)S(1)} %get-tuple-element.360), channel_id=1, source_target_pairs={{0,32},{32,64},{64,96},{96,128},{128,160},{160,192},{192,224},{224... | collective-permute-start | bytes 172040 | tf_op jit(solution)/shard_map/while/body/eval_jaxpr/ppermute | solution.py:12
  226.6 8.1 %copy-start = (s32[128]{0:T(128)S(1)}, s32[128]{0:T(128)}, u32[]{:S(2)}) copy-start(s32[128]{0:T(128)} %param.11) | copy-start | bytes 1540
  237.4 58.0 %all-to-all-start.2 = ((bf16[32,8,3584]{2,1,0:T(8,128)(2,1)}), bf16[32,8,3584]{2,1,0:T(8,128)(2,1)}, u32[]{:S(2)}, u32[]{:S(2)}) async-start(bf16[32,8,3584]{2,1,0:T(8,128)(2,1)} %fusion.8), calls=%async_computation.2 | async-start | bytes 3670016 | tf_op jit(solution)/shard_map/all_to_all | solution.py:93
  297.2 10.7 %collective-permute-start.1 = (bf16[8,3584]{1,0:T(8,128)(2,1)S(1)}, bf16[8,3584]{1,0:T(8,128)(2,1)S(1)}, u32[]{:S(2)}, u32[]{:S(2)}) collective-permute-start(bf16[8,3584]{1,0:T(8,128)(2,1)S(1)} %convert_element_type.82), channel_id=1, source_target_pairs={{0,32},{32,64},{64,96},{96,128},{128,160},{160,192},{192,224},{224... | collective-permute-start | bytes 172040 | tf_op jit(solution)/shard_map/while/body/eval_jaxpr/ppermute | solution.py:12
  308.1 8.2 %collective-permute-start.1 = (bf16[8,3584]{1,0:T(8,128)(2,1)S(1)}, bf16[8,3584]{1,0:T(8,128)(2,1)S(1)}, u32[]{:S(2)}, u32[]{:S(2)}) collective-permute-start(bf16[8,3584]{1,0:T(8,128)(2,1)S(1)} %convert_element_type.82), channel_id=1, source_target_pairs={{0,32},{32,64},{64,96},{96,128},{128,160},{160,192},{192,224},{224... | collective-permute-start | bytes 172040 | tf_op jit(solution)/shard_map/while/body/eval_jaxpr/ppermute | solution.py:12
  316.6 8.2 %collective-permute-start.1 = (bf16[8,3584]{1,0:T(8,128)(2,1)S(1)}, bf16[8,3584]{1,0:T(8,128)(2,1)S(1)}, u32[]{:S(2)}, u32[]{:S(2)}) collective-permute-start(bf16[8,3584]{1,0:T(8,128)(2,1)S(1)} %convert_element_type.82), channel_id=1, source_target_pairs={{0,32},{32,64},{64,96},{96,128},{128,160},{160,192},{192,224},{224... | collective-permute-start | bytes 172040 | tf_op jit(solution)/shard_map/while/body/eval_jaxpr/ppermute | solution.py:12
  325.0 8.2 %collective-permute-start.1 = (bf16[8,3584]{1,0:T(8,128)(2,1)S(1)}, bf16[8,3584]{1,0:T(8,128)(2,1)S(1)}, u32[]{:S(2)}, u32[]{:S(2)}) collective-permute-start(bf16[8,3584]{1,0:T(8,128)(2,1)S(1)} %convert_element_type.82), channel_id=1, source_target_pairs={{0,32},{32,64},{64,96},{96,128},{128,160},{160,192},{192,224},{224... | collective-permute-start | bytes 172040 | tf_op jit(solution)/shard_map/while/body/eval_jaxpr/ppermute | solution.py:12
  333.4 8.2 %collective-permute-start.1 = (bf16[8,3584]{1,0:T(8,128)(2,1)S(1)}, bf16[8,3584]{1,0:T(8,128)(2,1)S(1)}, u32[]{:S(2)}, u32[]{:S(2)}) collective-permute-start(bf16[8,3584]{1,0:T(8,128)(2,1)S(1)} %convert_element_type.82), channel_id=1, source_target_pairs={{0,32},{32,64},{64,96},{96,128},{128,160},{160,192},{192,224},{224... | collective-permute-start | bytes 172040 | tf_op jit(solution)/shard_map/while/body/eval_jaxpr/ppermute | solution.py:12
  341.9 8.4 %collective-permute-start.1 = (bf16[8,3584]{1,0:T(8,128)(2,1)S(1)}, bf16[8,3584]{1,0:T(8,128)(2,1)S(1)}, u32[]{:S(2)}, u32[]{:S(2)}) collective-permute-start(bf16[8,3584]{1,0:T(8,128)(2,1)S(1)} %convert_element_type.82), channel_id=1, source_target_pairs={{0,32},{32,64},{64,96},{96,128},{128,160},{160,192},{192,224},{224... | collective-permute-start | bytes 172040 | tf_op jit(solution)/shard_map/while/body/eval_jaxpr/ppermute | solution.py:12
  350.5 8.2 %collective-permute-start.1 = (bf16[8,3584]{1,0:T(8,128)(2,1)S(1)}, bf16[8,3584]{1,0:T(8,128)(2,1)S(1)}, u32[]{:S(2)}, u32[]{:S(2)}) collective-permute-start(bf16[8,3584]{1,0:T(8,128)(2,1)S(1)} %convert_element_type.82), channel_id=1, source_target_pairs={{0,32},{32,64},{64,96},{96,128},{128,160},{160,192},{192,224},{224... | collective-permute-start | bytes 172040 | tf_op jit(solution)/shard_map/while/body/eval_jaxpr/ppermute | solution.py:12
  358.9 8.2 %collective-permute-start.1 = (bf16[8,3584]{1,0:T(8,128)(2,1)S(1)}, bf16[8,3584]{1,0:T(8,128)(2,1)S(1)}, u32[]{:S(2)}, u32[]{:S(2)}) collective-permute-start(bf16[8,3584]{1,0:T(8,128)(2,1)S(1)} %convert_element_type.82), channel_id=1, source_target_pairs={{0,32},{32,64},{64,96},{96,128},{128,160},{160,192},{192,224},{224... | collective-permute-start | bytes 172040 | tf_op jit(solution)/shard_map/while/body/eval_jaxpr/ppermute | solution.py:12
  367.3 8.2 %collective-permute-start.1 = (bf16[8,3584]{1,0:T(8,128)(2,1)S(1)}, bf16[8,3584]{1,0:T(8,128)(2,1)S(1)}, u32[]{:S(2)}, u32[]{:S(2)}) collective-permute-start(bf16[8,3584]{1,0:T(8,128)(2,1)S(1)} %convert_element_type.82), channel_id=1, source_target_pairs={{0,32},{32,64},{64,96},{96,128},{128,160},{160,192},{192,224},{224... | collective-permute-start | bytes 172040 | tf_op jit(solution)/shard_map/while/body/eval_jaxpr/ppermute | solution.py:12
  375.8 8.2 %collective-permute-start.1 = (bf16[8,3584]{1,0:T(8,128)(2,1)S(1)}, bf16[8,3584]{1,0:T(8,128)(2,1)S(1)}, u32[]{:S(2)}, u32[]{:S(2)}) collective-permute-start(bf16[8,3584]{1,0:T(8,128)(2,1)S(1)} %convert_element_type.82), channel_id=1, source_target_pairs={{0,32},{32,64},{64,96},{96,128},{128,160},{160,192},{192,224},{224... | collective-permute-start | bytes 172040 | tf_op jit(solution)/shard_map/while/body/eval_jaxpr/ppermute | solution.py:12
  384.2 8.2 %collective-permute-start.1 = (bf16[8,3584]{1,0:T(8,128)(2,1)S(1)}, bf16[8,3584]{1,0:T(8,128)(2,1)S(1)}, u32[]{:S(2)}, u32[]{:S(2)}) collective-permute-start(bf16[8,3584]{1,0:T(8,128)(2,1)S(1)} %convert_element_type.82), channel_id=1, source_target_pairs={{0,32},{32,64},{64,96},{96,128},{128,160},{160,192},{192,224},{224... | collective-permute-start | bytes 172040 | tf_op jit(solution)/shard_map/while/body/eval_jaxpr/ppermute | solution.py:12
  392.6 8.2 %collective-permute-start.1 = (bf16[8,3584]{1,0:T(8,128)(2,1)S(1)}, bf16[8,3584]{1,0:T(8,128)(2,1)S(1)}, u32[]{:S(2)}, u32[]{:S(2)}) collective-permute-start(bf16[8,3584]{1,0:T(8,128)(2,1)S(1)} %convert_element_type.82), channel_id=1, source_target_pairs={{0,32},{32,64},{64,96},{96,128},{128,160},{160,192},{192,224},{224... | collective-permute-start | bytes 172040 | tf_op jit(solution)/shard_map/while/body/eval_jaxpr/ppermute | solution.py:12
  401.0 8.5 %collective-permute-start.1 = (bf16[8,3584]{1,0:T(8,128)(2,1)S(1)}, bf16[8,3584]{1,0:T(8,128)(2,1)S(1)}, u32[]{:S(2)}, u32[]{:S(2)}) collective-permute-start(bf16[8,3584]{1,0:T(8,128)(2,1)S(1)} %convert_element_type.82), channel_id=1, source_target_pairs={{0,32},{32,64},{64,96},{96,128},{128,160},{160,192},{192,224},{224... | collective-permute-start | bytes 172040 | tf_op jit(solution)/shard_map/while/body/eval_jaxpr/ppermute | solution.py:12
  409.7 8.2 %collective-permute-start.1 = (bf16[8,3584]{1,0:T(8,128)(2,1)S(1)}, bf16[8,3584]{1,0:T(8,128)(2,1)S(1)}, u32[]{:S(2)}, u32[]{:S(2)}) collective-permute-start(bf16[8,3584]{1,0:T(8,128)(2,1)S(1)} %convert_element_type.82), channel_id=1, source_target_pairs={{0,32},{32,64},{64,96},{96,128},{128,160},{160,192},{192,224},{224... | collective-permute-start | bytes 172040 | tf_op jit(solution)/shard_map/while/body/eval_jaxpr/ppermute | solution.py:12
  418.2 8.2 %collective-permute-start.1 = (bf16[8,3584]{1,0:T(8,128)(2,1)S(1)}, bf16[8,3584]{1,0:T(8,128)(2,1)S(1)}, u32[]{:S(2)}, u32[]{:S(2)}) collective-permute-start(bf16[8,3584]{1,0:T(8,128)(2,1)S(1)} %convert_element_type.82), channel_id=1, source_target_pairs={{0,32},{32,64},{64,96},{96,128},{128,160},{160,192},{192,224},{224... | collective-permute-start | bytes 172040 | tf_op jit(solution)/shard_map/while/body/eval_jaxpr/ppermute | solution.py:12
where the time goes:
time: 429 us; the launch traced here: 427 us
  waiting for transfers between devices  250 us (58%)
  starting transfers between devices  107 us (25%)
  local copies, waits for them, and re-layouts  34.6 us (8%)
  matrix products  23.3 us (5%)
  other arithmetic  10.7 us (2%)
    ppermute x30, waiting for transfers between devices, passed_along(): return lax.ppermute(value, axis, pairs)  188 us
    ppermute x30, starting transfers between devices, passed_along(): return lax.ppermute(value, axis, pairs)  77.7 us
    all_to_all x1, waiting for transfers between devices, body(): lax.all_to_all(part.reshape(nshard, rows_p, width), 'shard', split_axis=0...  37.5 us
    all_to_all x1, waiting for transfers between devices, body(): lax.all_to_all(served, 'shard', split_axis=0, concat_axis=0, tiled=True)  18.8 us
    gather x1, local copies, waits for them, and re-layouts, body(): hard_negative_rows = fetched.reshape(-1, width)[order_index]  17.8 us
    all_to_all x1, starting transfers between devices, body(): lax.all_to_all(requests, 'shard', split_axis=0, concat_axis=0, tiled=True)  12.6 us
    all_to_all x1, starting transfers between devices, body(): lax.all_to_all(part.reshape(nshard, rows_p, width), 'shard', split_axis=0...  10.6 us
  transfers between devices with their start and end apart: 33, of which 33 were waited for; matrix products, arithmetic and copies ran while one was open for 4% of the time, Pallas kernels for 0%

commit v1 on v0

v1 whole, which is shorter than its diff:
```python
import jax
import jax.numpy as jnp
from jax import lax
from jax.sharding import PartitionSpec as P

SOFTMAX_TEMP = 0.05


def body(queries, passages, positive, neg_owner, neg_row):
    nblk = lax.axis_size("blk")
    nshard = lax.axis_size("shard")
    qb = queries.astype(jnp.bfloat16)
    pb = passages.astype(jnp.bfloat16)
    rows_p, width = pb.shape
    group = nblk * rows_p
    bank_rows = nshard * rows_p
    bank = lax.all_gather(pb, "shard", axis=0, tiled=True)
    members = lax.all_gather(pb, "blk", axis=0, tiled=True)
    index = neg_owner * rows_p + neg_row
    columns = jnp.arange(bank_rows, dtype=jnp.int32)
    named = jnp.any(index[:, :, None] == columns[None, None, :], axis=1)
    hit = jnp.arange(group, dtype=jnp.int32)[None, :] == positive[:, None]
    s_hn = jnp.einsum("qd,pd->qp", qb, bank, preferred_element_type=jnp.float32) / SOFTMAX_TEMP
    s_in = jnp.einsum("qd,pd->qp", qb, members, preferred_element_type=jnp.float32) / SOFTMAX_TEMP
    s_hn = jnp.where(named, s_hn, -jnp.inf)
    top = jnp.maximum(jnp.max(s_in, -1), jnp.max(s_hn, -1))
    total = jnp.sum(jnp.exp(s_in - top[:, None]), -1) + jnp.sum(jnp.exp(s_hn - top[:, None]), -1)
    lse = top + jnp.log(total)
    losses = lse - jnp.sum(jnp.where(hit, s_in, jnp.float32(0.0)), -1)
    w_in = (jnp.exp(s_in - lse[:, None]) - hit.astype(jnp.float32)).astype(jnp.bfloat16)
    w_hn = jnp.exp(s_hn - lse[:, None]).astype(jnp.bfloat16)
    part = jnp.einsum("qc,qd->cd", w_hn, qb, preferred_element_type=jnp.float32) / SOFTMAX_TEMP
    term = jnp.einsum("qc,qd->cd", w_in, qb, preferred_element_type=jnp.float32) / SOFTMAX_TEMP
    hard_grad = lax.psum_scatter(part.astype(jnp.bfloat16), "shard", scatter_dimension=0, tiled=True)
    group_grad = lax.psum_scatter(term.astype(jnp.bfloat16), "blk", scatter_dimension=0, tiled=True)
    query_gradient = (
        jnp.einsum("qp,pd->qd", w_in, members, preferred_element_type=jnp.float32)
        + jnp.einsum("qp,pd->qd", w_hn, bank, preferred_element_type=jnp.float32)
    ) / SOFTMAX_TEMP
    passage_gradient = hard_grad.astype(jnp.float32) + group_grad.astype(jnp.float32)
    return (query_gradient, passage_gradient, losses)


def solution(mesh):
    rows = P(("blk", "shard"), None)
    flat = P(("blk", "shard"))
    return jax.shard_map(
        body,
        mesh=mesh,
        in_specs=(rows, rows, flat, rows, rows),
        out_specs=(rows, rows, flat),
        check_vma=False,
    )
```

time: 429 us -> 316 us (0.74)
  the two profiles are of different devices: /device:TPU:64 before, /device:TPU:1 now
where the time goes in v1:
time: 316 us; the launch traced here: 312 us
  waiting for transfers between devices  249 us (79%)
  blocking collectives  33.9 us (11%)
  between operations  13.8 us (4%)
  matrix products  8.1 us (3%)
  other arithmetic  5.58 us (2%)
    reduce_scatter x1, waiting for transfers between devices, body(): lax.psum_scatter(part.astype(jnp.bfloat16), 'shard', scatter_dimension=0,...  137 us
    all_gather x1, waiting for transfers between devices, body(): bank = lax.all_gather(pb, 'shard', axis=0, tiled=True)  58.1 us
    reduce_scatter x1, waiting for transfers between devices, body(): lax.psum_scatter(term.astype(jnp.bfloat16), 'blk', scatter_dimension=0, t...  53.6 us
    all_gather x1, blocking collectives, body(): members = lax.all_gather(pb, 'blk', axis=0, tiled=True)  33.9 us
  transfers between devices with their start and end apart: 3, of which 3 were waited for; matrix products, arithmetic and copies ran while one was open for 2% of the time, Pallas kernels for 0%

profile of v1, /device:TPU:1, one launch (start us, length us, event | category | flops | bytes accessed | tf_op | source)
XLA Modules:
  0.0 311.8 jit_solution(8536600057212841868)
XLA Ops:
  7.2 0.0 copy-start.3
  7.2 0.0 copy-start.4
  7.2 0.0 all-gather.2.cloned.1.call-start
  7.2 1.5 convert_element_type.28
  8.8 0.0 copy-start.1
  8.8 0.0 all-gather.2.cloned.1.call-update
  8.8 0.0 reduce-scatter.5.cloned.1.call-start
  8.8 1.6 convert_element_type.27
  10.4 0.0 copy-done.3
  10.4 0.0 copy-done.4
  10.5 0.2 fusion.4
  10.7 0.0 copy-done.1
  10.7 33.9 %all_gather.6 = bf16[128,3584]{1,0:T(8,128)(2,1)S(1)} all-gather(bf16[8,3584]{1,0:T(8,128)(2,1)S(1)} %copy-done.1), channel_id=1, replica_groups=mesh['blk'=16,'shard'=32] {'blk'}, dimensions={0}, use_global_device_ids=true | all-gather | bytes 974848 | tf_op jit(solution)/shard_map/all_gather | solution.py:18
  44.6 0.4 fusion.7
  45.0 0.0 copy-start.2
  45.0 58.1 %all-gather.2.cloned.1.call-done = bf16[256,3584]{1,0:T(8,128)(2,1)} async-done(((bf16[8,3584]{1,0:T(8,128)(2,1)}), bf16[256,3584]{1,0:T(8,128)(2,1)}) %all-gather.2.cloned.1.call-update) | async-done | bytes 1835024 | tf_op jit(solution)/shard_map/all_gather | solution.py:17
  103.1 2.3 fusion.8
  105.4 0.2 exponential_reduce_fusion
  105.6 0.0 copy-done.2
  105.6 0.5 fusion.6
  106.2 1.3 fusion.2
  107.5 0.0 reduce-scatter.5.cloned.1.call-update
  107.5 0.0 reduce-scatter.3.cloned.1.call-start
  107.5 2.0 fusion
  109.5 0.0 reduce-scatter.3.cloned.1.call-update
  109.5 0.0 copy-start
  109.5 0.4 fusion.5
  110.0 1.1 copy-done
  111.0 1.7 fusion.1
  112.7 53.6 %reduce-scatter.5.cloned.1.call-done = bf16[8,3584]{1,0:T(8,128)(2,1)} async-done(((bf16[128,3584]{1,0:T(8,128)(2,1)}), bf16[8,3584]{1,0:T(8,128)(2,1)}) %reduce-scatter.5.cloned.1.call-update) | async-done | bytes 57360 | tf_op jit(solution)/shard_map/reduce_scatter | solution.py:35
  166.3 137.5 %reduce-scatter.3.cloned.1.call-done = bf16[8,3584]{1,0:T(8,128)(2,1)} async-done(((bf16[256,3584]{1,0:T(8,128)(2,1)}), bf16[8,3584]{1,0:T(8,128)(2,1)}) %reduce-scatter.3.cloned.1.call-update) | async-done | bytes 57360 | tf_op jit(solution)/shard_map/reduce_scatter | solution.py:34
  303.8 1.5 convert_add_fusion
  (3 shorter events, 0.1 us)
Async XLA Ops:
  7.2 3.3 %copy-start.3 = (s32[128,7]{0,1:T(8,128)S(1)}, s32[128,7]{0,1:T(8,128)}, u32[]{:S(2)}) copy-start(s32[128,7]{0,1:T(8,128)} %param.9) | copy-start | bytes 10756
  7.2 3.3 %copy-start.4 = (s32[128,7]{0,1:T(8,128)S(1)}, s32[128,7]{0,1:T(8,128)}, u32[]{:S(2)}) copy-start(s32[128,7]{0,1:T(8,128)} %param.8) | copy-start | bytes 10756
  7.2 95.9 %all-gather.2.cloned.1.call-start = ((), (), s32[]{:S(2)}) async-start(), calls=%async_computation.2 | async-start | bytes 1892352 | tf_op jit(solution)/shard_map/all_gather | solution.py:17
  8.8 1.9 copy-start.1
  8.8 157.5 %reduce-scatter.5.cloned.1.call-start = ((), (), s32[]{:S(2)}) async-start(), calls=%async_computation.4 | async-start | bytes 974848 | tf_op jit(solution)/shard_map/reduce_scatter | solution.py:35
  45.0 60.6 %copy-start.2 = (s32[128]{0:T(128)S(1)}, s32[128]{0:T(128)}, u32[]{:S(2)}) copy-start(s32[128]{0:T(128)} %param.7) | copy-start | bytes 1540
  107.5 196.3 %reduce-scatter.3.cloned.1.call-start = ((), (), s32[]{:S(2)}) async-start(), calls=%async_computation.3 | async-start | bytes 1892352 | tf_op jit(solution)/shard_map/reduce_scatter | solution.py:34
  109.5 1.5 copy-start
Sparse Core Ops, SparseCore 0:
  11.9 91.0 all-gather.1
  107.6 58.6 reduce-scatter.4
  171.7 132.0 reduce-scatter.2

commit v2 on v1

v2 whole, which is shorter than its diff:
```python
import functools

import jax
import jax.numpy as jnp
from jax import lax
from jax.experimental import pallas as pl
from jax.experimental.pallas import tpu as pltpu
from jax.sharding import PartitionSpec as P

SCALE = 20.0
NONE = -1e30
MESH = pl.DeviceIdType.MESH
F32, BF16, I32 = jnp.float32, jnp.bfloat16, jnp.int32


def stacked(wide):
    half = wide.shape[1] // 2
    return jnp.concatenate([wide[:, :half], wide[:, half:]], axis=0)


def gather_lists(n):
    half = n // 2
    plus = [list(range(n - 1, half - 1 + kind, -1)) for kind in (0, 1)]
    minus = [list(range(1, half + kind)) for kind in (0, 1)]
    return plus, minus


def scatter_lists(n):
    half = n // 2
    plus = [(half, 0)]
    for r in range(half - 1, 0, -1):
        plus += [(r, 1), (r, 0)]
    minus = []
    for r in range(half - 1, 0, -1):
        minus += [(r, 0), (r + 1, 1)]
    minus.append((1, 1))
    return plus, minus


def kernel(
    nblk, nshard,
    q_hbm, p_hbm, pos_ref, owner_ref, row_ref,
    qg_hbm, pg_ref, loss_ref,
    qf, pf, q2, hbuf, gbuf, bank, sh, sg, bias, codes, codes_in, lse_out, lse_in,
    part_h, part_g, hs, hr, gs, gr, xs, xr, qs, qr,
    local_sem, ag_s, ag_r, xa_s, xa_r, core_s, core_r, rs_s, rs_r, xb_s, xb_r,
):
    ny, nz = nblk // 2, nshard // 4
    b, s = lax.axis_index("blk"), lax.axis_index("shard")
    y, xl = lax.div(b, 2), lax.rem(b, 2)
    xh, z, c = lax.div(s, 2 * nz), lax.rem(lax.div(s, 2), nz), lax.rem(s, 2)

    def device(y_, xl_, xh_, z_, c_):
        return (y_ * 2 + xl_, xh_ * (2 * nz) + z_ * 2 + c_)

    next_z = device(y, xl, xh, lax.rem(z + 1, nz), c)
    prev_z = device(y, xl, xh, lax.rem(z + nz - 1, nz), c)
    next_y = device(lax.rem(y + 1, ny), xl, xh, z, c)
    prev_y = device(lax.rem(y + ny - 1, ny), xl, xh, z, c)
    other_xh = device(y, xl, 1 - xh, z, c)
    other_xl = device(y, 1 - xl, xh, z, c)
    other_core = device(y, xl, xh, z, 1 - c)
    rings = (
        (nz, (next_z, prev_z), hbuf, other_xh, hs, hr, part_h),
        (ny, (next_y, prev_y), gbuf, other_xl, gs, gr, part_g),
    )
    rows_q, width = qf.shape
    rows_h, rows_g = 16 * nz, 16 * ny
    wh = width // 2
    quarter = width // 4

    def send(src, dst, ssem, rsem, to):
        copy = pltpu.make_async_remote_copy(
            src_ref=src, dst_ref=dst, send_sem=ssem, recv_sem=rsem, device_id=to, device_id_type=MESH
        )
        copy.start()
        return copy

    sent = []
    p_copy = pltpu.make_async_copy(p_hbm, pf, local_sem.at[0])
    p_copy.start()
    q_copy = pltpu.make_async_copy(q_hbm, qf, local_sem.at[1])
    q_copy.start()
    barrier = pltpu.get_barrier_semaphore()
    for to in (next_z, prev_z, next_y, prev_y, other_xh, other_xl, other_core):
        pl.semaphore_signal(barrier, inc=1, device_id=to, device_id_type=MESH)
    p_copy.wait()
    mine = stacked(pf[...]).astype(BF16)
    hbuf[0, 0] = mine
    gbuf[0, 0] = mine
    pl.semaphore_wait(barrier, 7)

    arrive = [{}, {}]
    for i, (n, near, buf, cross, _, _, _) in enumerate(rings):
        arrive[i][(0, 1)] = send(buf.at[0, 0], buf.at[0, 1], xa_s.at[i], xa_r.at[i], cross)
    lists = [gather_lists(ring[0]) for ring in rings]

    def gather_send(i, d, kind, step):
        n, near, buf = rings[i][:3]
        slots = lists[i][d][kind]
        if step >= len(slots):
            return
        dst = slots[step]
        src = 0 if step == 0 else slots[step - 1]
        if (src, kind) != (0, 0) and (src, kind) not in done[i]:
            arrive[i][(src, kind)].wait_recv()
            done[i].add((src, kind))
        arrive[i][(dst, kind)] = send(
            buf.at[src, kind], buf.at[dst, kind], ag_s.at[i, dst, kind], ag_r.at[i, dst, kind], near[d]
        )

    done = [{(0, 0)}, {(0, 0)}]
    for i in (0, 1):
        for d in (0, 1):
            gather_send(i, d, 0, 0)

    q_copy.wait()
    q2[0:rows_q, :] = qf[...].astype(BF16)
    q_send = send(
        q2.at[pl.ds(0, rows_q)], q2.at[pl.ds(rows_q, rows_q)], core_s.at[0], core_r.at[0], other_core
    )
    for i in (0, 1):
        for d in (0, 1):
            gather_send(i, d, 1, 0)
    shift_z, shift_y = max(nz // 2 - 2, 0), max(ny // 2 - 2, 0)
    negs = owner_ref.shape[0]
    owner_t, row_t = owner_ref[...], row_ref[...]
    place = ((owner_t >> 1) - z + (nz + shift_z)) & (nz - 1)
    cross_bit = (owner_t >= 2 * nz).astype(I32) ^ xh
    column = place * 16 + cross_bit * 8 + row_t
    same_core = (owner_t & 1) == c
    codes[0, 0:negs, :] = jnp.where(same_core, column, -1)
    codes[1, 0:negs, :] = jnp.where(same_core, -1, column)
    codes[1, negs:8, :] = jnp.full((8 - negs, rows_q), -1, I32)
    code_send = send(codes.at[1], codes_in, core_s.at[1], core_r.at[1], other_core)
    sent += [q_send, code_send]
    row_ids = lax.broadcasted_iota(I32, (rows_h, rows_q), 0)

    def bias_of(code):
        named = row_ids == code[0:1, :]
        for k in range(1, negs):
            named = named | (row_ids == code[k : k + 1, :])
        return jnp.where(named, jnp.float32(0.0), jnp.float32(NONE))

    bias[:, 0:rows_q] = bias_of(codes[0, 0:negs, :])
    p = pos_ref[...]
    g_column = (((p >> 4) - y + (ny + shift_y)) & (ny - 1)) * 16 + (((p >> 3) & 1) ^ xl) * 8 + (p & 7)
    hit = lax.broadcasted_iota(I32, (rows_g, rows_q), 0) == g_column

    base = (0, rows_h)
    shifts = (shift_z, shift_y)

    def place_of(i, slot):
        return (slot + shifts[i]) % rings[i][0]

    def assemble(i, slot):
        buf = rings[i][2]
        for kind in (0, 1):
            if (slot, kind) not in done[i]:
                arrive[i][(slot, kind)].wait_recv()
                done[i].add((slot, kind))
        first, second = buf[slot, 0].astype(F32), buf[slot, 1].astype(F32)
        at = base[i] + 16 * place_of(i, slot)
        bank[at : at + 16, 0:wh] = jnp.concatenate([first[0:8], second[0:8]], axis=0).astype(BF16)
        bank[at : at + 16, wh:width] = jnp.concatenate([first[8:16], second[8:16]], axis=0).astype(BF16)

    def scores(i, start, stop):
        if stop <= start:
            return
        rows = bank[base[i] + 16 * start : base[i] + 16 * stop, :]
        queries = q2[...] if i == 0 else q2[0:rows_q, :]
        out = lax.dot_general(rows, queries, (((1,), (1,)), ((), ())), preferred_element_type=F32) * SCALE
        if i == 0:
            sh[16 * start : 16 * stop, :] = out
        else:
            sg[16 * start : 16 * stop, :] = out

    rounds = max(nz, ny) // 2
    for step in range(1, rounds):
        for kind in (0, 1):
            for i in (0, 1):
                for d in (0, 1):
                    gather_send(i, d, kind, step)
    early = [max(2 * (ring[0] // 2 - 2) + 1, 0) for ring in rings]
    for i in (0, 1):
        for at in range(early[i]):
            assemble(i, (at - shifts[i]) % rings[i][0])
    q_send.wait_recv()
    for i in (0, 1):
        scores(i, 0, early[i])
    code_send.wait_recv()
    bias[:, rows_q : 2 * rows_q] = bias_of(codes_in[...])
    for i in (0, 1):
        for at in range(early[i], rings[i][0]):
            assemble(i, (at - shifts[i]) % rings[i][0])
    for i in (0, 1):
        scores(i, early[i], rings[i][0])

    s_g = sg[...]
    s_h = sh[...] + bias[...]
    s_own, s_par = s_h[:, 0:rows_q], s_h[:, rows_q : 2 * rows_q]
    top_own = jnp.maximum(jnp.max(s_g, 0, keepdims=True), jnp.max(s_own, 0, keepdims=True))
    sum_own = jnp.sum(jnp.exp(s_g - top_own), 0, keepdims=True) + jnp.sum(
        jnp.exp(s_own - top_own), 0, keepdims=True
    )
    top_par = jnp.max(s_par, 0, keepdims=True)
    sum_par = jnp.sum(jnp.exp(s_par - top_par), 0, keepdims=True)
    lse_out[0:1, :] = top_own
    lse_out[1:2, :] = sum_own
    lse_out[2:3, :] = top_par
    lse_out[3:4, :] = sum_par
    lse_out[4:8, :] = jnp.zeros((4, rows_q), F32)
    lse_send = send(lse_out, lse_in, core_s.at[2], core_r.at[2], other_core)
    sent.append(lse_send)
    chosen = jnp.sum(jnp.where(hit, s_g, jnp.float32(0.0)), 0, keepdims=True)
    lse_send.wait_recv()

    def joined(top_a, sum_a, top_b, sum_b):
        top = jnp.maximum(top_a, top_b)
        return top + jnp.log(sum_a * jnp.exp(top_a - top) + sum_b * jnp.exp(top_b - top))

    lse = joined(top_own, sum_own, lse_in[2:3, :], lse_in[3:4, :])
    lse_par = joined(lse_in[0:1, :], lse_in[1:2, :], top_par, sum_par)
    loss_ref[...] = lse - chosen
    w_g = jnp.exp(s_g - lse) - hit.astype(F32)
    w_own = jnp.exp(s_own - lse)
    w_par = jnp.exp(s_par - lse_par)
    w_h = jnp.concatenate([w_own, w_par], axis=1).astype(BF16)
    w_gb = w_g.astype(BF16)

    out_lists = [scatter_lists(ring[0]) for ring in rings]
    coming = [{}, {}]

    def terms(h):
        cols = slice(h * wh, (h + 1) * wh)
        part_h[:, cols] = jnp.dot(w_h, q2[:, cols], preferred_element_type=F32) * SCALE
        part_g[:, cols] = jnp.dot(w_gb, q2[0:rows_q, cols], preferred_element_type=F32) * SCALE

    def own_term(i, slot, h):
        at = 16 * place_of(i, slot)
        return rings[i][6][at : at + 16, h * wh : (h + 1) * wh]

    def scatter_send(i, d, step):
        n, near, _, _, out, into, _ = rings[i]
        if step >= len(out_lists[i][d]):
            return
        r, h = out_lists[i][d][step]
        value = own_term(i, r if d == 0 else n - r, h)
        if (d, r, h) in coming[i]:
            coming[i][(d, r, h)].wait_recv()
            value = value + into[d, r, h].astype(F32)
        out[d, r, h] = value.astype(BF16)
        copy = send(
            out.at[d, r, h], into.at[d, r - 1, h], rs_s.at[i, d, r, h], rs_r.at[i, d, r - 1, h], near[d]
        )
        coming[i][(d, r - 1, h)] = copy
        sent.append(copy)

    def all_dirs(step):
        for i in (0, 1):
            for d in (0, 1):
                scatter_send(i, d, step)

    terms(0)
    if nz == 8 and ny == 8:
        all_dirs(0)
        terms(1)
    else:
        terms(1)
        all_dirs(0)
    all_dirs(1)
    w_par_q = jnp.transpose(w_par).astype(BF16)
    w_own_q = jnp.concatenate([jnp.transpose(w_own), jnp.transpose(w_g)], axis=1).astype(BF16)
    for h in (0, 1):
        cols = slice(h * wh, (h + 1) * wh)
        qs[:, cols] = (jnp.dot(w_par_q, bank[0:rows_h, cols], preferred_element_type=F32) * SCALE).astype(BF16)
    qg_send = send(qs, qr, core_s.at[3], core_r.at[3], other_core)
    sent.append(qg_send)
    all_dirs(2)
    for h in (0, 1):
        cols = slice(h * wh, (h + 1) * wh)
        qf[:, cols] = jnp.dot(w_own_q, bank[:, cols], preferred_element_type=F32) * SCALE
    all_dirs(3)
    qg_send.wait_recv()
    qf[...] = qf[...] + qr[...].astype(F32)
    qg_copy = pltpu.make_async_copy(qf, qg_hbm, local_sem.at[2])
    qg_copy.start()
    for step in range(4, max(len(l) for lists_ in out_lists for l in lists_)):
        all_dirs(step)

    crossing, totals = {}, {}
    for h in (0, 1):
        for i in (0, 1):
            total = own_term(i, 0, h)
            for d in (0, 1):
                if (d, 0, h) in coming[i]:
                    coming[i][(d, 0, h)].wait_recv()
                    total = total + rings[i][5][d, 0, h].astype(F32)
            xs[i, h] = stacked(total[8:16]).astype(BF16)
            crossing[i, h] = send(xs.at[i, h], xr.at[i, h], xb_s.at[i, h], xb_r.at[i, h], rings[i][3])
            sent.append(crossing[i, h])
            totals[i, h] = total[0:8]
    for h in (0, 1):
        total = totals[0, h] + totals[1, h]
        crossing[0, h].wait_recv()
        crossing[1, h].wait_recv()
        over = xr[0, h].astype(F32) + xr[1, h].astype(F32)
        pg_ref[:, h * wh : h * wh + quarter] = total[:, 0:quarter] + over[0:8]
        pg_ref[:, h * wh + quarter : (h + 1) * wh] = total[:, quarter:wh] + over[8:16]
    for i in (0, 1):
        for copy in arrive[i].values():
            copy.wait_send()
    for copy in sent:
        copy.wait_send()
    qg_copy.wait()


def body(queries, passages, positive, neg_owner, neg_row):
    nblk, nshard = lax.axis_size("blk"), lax.axis_size("shard")
    ny, nz = nblk // 2, nshard // 4
    rows_q, width = queries.shape
    rows_p = passages.shape[0]
    wh = width // 2
    vmem = pl.BlockSpec(memory_space=pltpu.VMEM)
    anywhere = pl.BlockSpec(memory_space=pl.ANY)
    dma = pltpu.SemaphoreType.DMA
    top = max(ny, nz)
    scratch = [
        pltpu.VMEM((rows_q, width), F32),
        pltpu.VMEM((rows_p, width), F32),
        pltpu.VMEM((2 * rows_q, width), BF16),
        pltpu.VMEM((nz, 2, 16, wh), BF16),
        pltpu.VMEM((ny, 2, 16, wh), BF16),
        pltpu.VMEM((16 * (nz + ny), width), BF16),
        pltpu.VMEM((16 * nz, 2 * rows_q), F32),
        pltpu.VMEM((16 * ny, rows_q), F32),
        pltpu.VMEM((16 * nz, 2 * rows_q), F32),
        pltpu.VMEM((2, 8, rows_q), I32),
        pltpu.VMEM((8, rows_q), I32),
        pltpu.VMEM((8, rows_q), F32),
        pltpu.VMEM((8, rows_q), F32),
        pltpu.VMEM((16 * nz, width), F32),
        pltpu.VMEM((16 * ny, width), F32),
        pltpu.VMEM((2, nz // 2 + 1, 2, 16, wh), BF16),
        pltpu.VMEM((2, nz // 2, 2, 16, wh), BF16),
        pltpu.VMEM((2, ny // 2 + 1, 2, 16, wh), BF16),
        pltpu.VMEM((2, ny // 2, 2, 16, wh), BF16),
        pltpu.VMEM((2, 2, 16, wh // 2), BF16),
        pltpu.VMEM((2, 2, 16, wh // 2), BF16),
        pltpu.VMEM((rows_q, width), BF16),
        pltpu.VMEM((rows_q, width), BF16),
        dma((3,)),
        dma((2, top, 2)), dma((2, top, 2)),
        dma((2,)), dma((2,)),
        dma((4,)), dma((4,)),
        dma((2, 2, top // 2 + 1, 2)), dma((2, 2, top // 2 + 1, 2)),
        dma((2, 2)), dma((2, 2)),
    ]
    qg, pg, loss = pl.pallas_call(
        functools.partial(kernel, nblk, nshard),
        out_shape=(
            jax.ShapeDtypeStruct((rows_q, width), F32),
            jax.ShapeDtypeStruct((rows_p, width), F32),
            jax.ShapeDtypeStruct((1, rows_q), F32),
        ),
        in_specs=[anywhere, anywhere, vmem, vmem, vmem],
        out_specs=(anywhere, vmem, vmem),
        scratch_shapes=scratch,
        compiler_params=pltpu.CompilerParams(
            collective_id=0, has_side_effects=True, vmem_limit_bytes=40 * 1024 * 1024
        ),
    )(queries, passages, positive.reshape(1, rows_q), neg_owner.T, neg_row.T)
    return (qg, pg, loss.reshape(rows_q))


def solution(mesh):
    rows = P(("blk", "shard"), None)
    flat = P(("blk", "shard"))
    return jax.shard_map(
        body,
        mesh=mesh,
        in_specs=(rows, rows, flat, rows, rows),
        out_specs=(rows, rows, flat),
        check_vma=False,
    )
```

time: 316 us -> 62.3 us (0.20); the launches traced: 312 us -> 61.5 us
  waiting for transfers between devices: 249 us -> 0 us
  Pallas kernels: 0 us -> 54.1 us
  blocking collectives: 33.9 us -> 0 us
  between operations: 13.8 us -> 0.65 us
  matrix products: 8.1 us -> 0 us
  local copies, waits for them, and re-layouts: 1.08 us -> 6.81 us
  other arithmetic: 5.58 us -> 0 us
    reduce_scatter x2 -> x0, waiting for transfers between devices: 191 us -> none  [the longest x1 137 us: body(): lax.psum_scatter(part.astype(jnp.bfloat16), 'shard', scatter_dimension=0,...]
    all_gather x1 -> x0, waiting for transfers between devices: 58.1 us -> none  [body(): bank = lax.all_gather(pb, 'shard', axis=0, tiled=True)]
    pallas_call x0 -> x1, Pallas kernels: none -> 54.1 us  [body(): pl.pallas_call(functools.partial(kernel, nblk, nshard), out_shape=(jax.Sh...]
    all_gather x1 -> x0, blocking collectives: 33.9 us -> none  [body(): members = lax.all_gather(pb, 'blk', axis=0, tiled=True)]
    dot_general x6 -> x0, matrix products: 8.1 us -> none  [the longest x1 2.29 us: body(): jnp.einsum('qd,pd->qp', qb, bank, preferred_element_type=jnp.float32)]
    unnamed x10 -> x13, local copies, waits for them, and re-layouts: 1.08 us -> 6.81 us
  transfers between devices with their start and end apart: 3 -> 0, of which waited for: 3 -> 0; matrix products, arithmetic and copies ran while one was open for 2% -> 0% of each run, Pallas kernels for 0% -> 0%
where the time goes in v2:
time: 62.3 us; the launch traced here: 61.5 us
  Pallas kernels  54.1 us (87%)
  local copies, waits for them, and re-layouts  6.81 us (11%)
  between operations  0.65 us (1%)
    pallas_call x1, Pallas kernels, body(): pl.pallas_call(functools.partial(kernel, nblk, nshard), out_shape=(jax.Sh...  54.1 us
    unnamed x13, local copies, waits for them, and re-layouts  6.81 us

profile of v2, /device:TPU:1, one launch (start us, length us, event | category | flops | bytes accessed | tf_op | source)
XLA Modules:
  0.0 61.5 jit_solution(14638256347323605335)
XLA Ops:
  0.6 0.0 copy-start
  0.6 1.5 %copy-done = f32[128,3584]{1,0:T(8,128)S(1)} copy-done((f32[128,3584]{1,0:T(8,128)S(1)}, f32[128,3584]{1,0:T(8,128)}, u32[]{:S(2)}) %copy-start) | copy-done | bytes 1835032
  2.1 0.0 copy-start.1
  2.1 0.9 %copy-done.1 = f32[8,3584]{1,0:T(8,128)S(1)} copy-done((f32[8,3584]{1,0:T(8,128)S(1)}, f32[8,3584]{1,0:T(8,128)}, u32[]{:S(2)}) %copy-start.1) | copy-done | bytes 114712
  3.0 0.0 copy-start.2
  3.0 0.7 %copy-done.2 = s32[128,7]{0,1:T(8,128)S(1)} copy-done((s32[128,7]{0,1:T(8,128)S(1)}, s32[128,7]{0,1:T(8,128)}, u32[]{:S(2)}) %copy-start.2) | copy-done | bytes 3608
  3.7 0.0 copy-start.3
  3.7 0.7 %copy-done.3 = s32[128,7]{0,1:T(8,128)S(1)} copy-done((s32[128,7]{0,1:T(8,128)S(1)}, s32[128,7]{0,1:T(8,128)}, u32[]{:S(2)}) %copy-start.3) | copy-done | bytes 3608
  4.4 0.0 copy-start.4
  4.4 0.7 %copy-done.4 = s32[128]{0:T(128)S(1)} copy-done((s32[128]{0:T(128)S(1)}, s32[128]{0:T(128)}, u32[]{:S(2)}) %copy-start.4) | copy-done | bytes 536
  5.1 54.1 %shard_map.76 = (f32[128,3584]{1,0:T(8,128)S(1)}, f32[8,3584]{1,0:T(8,128)S(1)}, f32[1,128]{1,0:T(1,128)S(1)}) custom-call(f32[128,3584]{1,0:T(8,128)S(1)} %copy-done, f32[8,3584]{1,0:T(8,128)S(1)} %copy-done.1, s32[1,128]{1,0:T(1,128)S(1)} %bitcast.6, s32[7,128]{1,0:T(8,128)S(1)} %bitcast.4, s32[7,128]{1,0:T(8,128)S(1)} %bitcast.5), custom_call_target="tpu_custom_call" | custom-call | tf_op jit(solution)/shard_map/pallas_call | solution.py:359
  59.1 1.2 %copy.11 = f32[128,3584]{1,0:T(8,128)} copy(f32[128,3584]{1,0:T(8,128)S(1)} %get-tuple-element.12) | data formatting | bytes 3670016
  60.4 0.6 %copy.12 = f32[8,3584]{1,0:T(8,128)} copy(f32[8,3584]{1,0:T(8,128)S(1)} %get-tuple-element.13) | data formatting | bytes 229376
  61.0 0.5 copy.13
Async XLA Ops:
  0.6 1.5 %copy-start = (f32[128,3584]{1,0:T(8,128)S(1)}, f32[128,3584]{1,0:T(8,128)}, u32[]{:S(2)}) copy-start(f32[128,3584]{1,0:T(8,128)} %q_hbm.1) | copy-start | bytes 5505028
  2.1 0.9 %copy-start.1 = (f32[8,3584]{1,0:T(8,128)S(1)}, f32[8,3584]{1,0:T(8,128)}, u32[]{:S(2)}) copy-start(f32[8,3584]{1,0:T(8,128)} %p_hbm.1) | copy-start | bytes 344068
  3.0 0.7 %copy-start.2 = (s32[128,7]{0,1:T(8,128)S(1)}, s32[128,7]{0,1:T(8,128)}, u32[]{:S(2)}) copy-start(s32[128,7]{0,1:T(8,128)} %param.8) | copy-start | bytes 10756
  3.7 0.7 %copy-start.3 = (s32[128,7]{0,1:T(8,128)S(1)}, s32[128,7]{0,1:T(8,128)}, u32[]{:S(2)}) copy-start(s32[128,7]{0,1:T(8,128)} %param.9) | copy-start | bytes 10756
  4.4 0.7 %copy-start.4 = (s32[128]{0:T(128)S(1)}, s32[128]{0:T(128)}, u32[]{:S(2)}) copy-start(s32[128]{0:T(128)} %param.7) | copy-start | bytes 1540

commit v3 on v2

v3 whole, which is shorter than its diff:
```python
import functools

import jax
import jax.numpy as jnp
from jax import lax
from jax.experimental import pallas as pl
from jax.experimental.pallas import tpu as pltpu
from jax.sharding import PartitionSpec as P

SCALE = 20.0
NONE = -1e30
MESH = pl.DeviceIdType.MESH
F32, BF16, I32 = jnp.float32, jnp.bfloat16, jnp.int32


def stacked(wide):
    half = wide.shape[1] // 2
    return jnp.concatenate([wide[:, :half], wide[:, half:]], axis=0)


def tree(n, kind):
    half = n // 2
    direct = 2 if half > 2 else 1
    edges = []
    for d in range(direct, 0, -1):
        if d < half:
            edges += [(0, d), (0, -d)]
    for d in range(direct + 1, half):
        edges += [(1 - d, 1), (d - 1, -1)]
    edges.append((1 - half, 1) if kind == 0 else (half - 1, -1))
    return edges


def kernel(
    nblk, nshard,
    q_hbm, p_hbm, pos_hbm, owner_hbm, row_hbm,
    qg_ref, pg_ref, loss_ref,
    qf, pf, pos_ref, owner_ref, row_ref, q2, hbuf, gbuf, bank, sh, sg, bias, codes, codes_in, lse_out, lse_in,
    part_h, part_g, hs, hr, gs, gr, xs, xr, qs, qr,
    local_sem, ag_s, ag_r, xa_s, xa_r, core_s, core_r, rs_s, rs_r, xb_s, xb_r,
):
    ny, nz = nblk // 2, nshard // 4
    b, s = lax.axis_index("blk"), lax.axis_index("shard")
    y, xl = lax.div(b, 2), lax.rem(b, 2)
    xh, z, c = lax.div(s, 2 * nz), lax.rem(lax.div(s, 2), nz), lax.rem(s, 2)

    def device(y_, xl_, xh_, z_, c_):
        return (y_ * 2 + xl_, xh_ * (2 * nz) + z_ * 2 + c_)

    def along_z(jump):
        return device(y, xl, xh, lax.rem(z + (jump + nz), nz), c)

    def along_y(jump):
        return device(lax.rem(y + (jump + ny), ny), xl, xh, z, c)

    other_xh = device(y, xl, 1 - xh, z, c)
    other_xl = device(y, 1 - xl, xh, z, c)
    other_core = device(y, xl, xh, z, 1 - c)
    rings = (
        (nz, along_z, hbuf, other_xh, hs, hr, part_h),
        (ny, along_y, gbuf, other_xl, gs, gr, part_g),
    )
    trees = [[tree(ring[0], kind) for kind in (0, 1)] for ring in rings]
    partners = {}
    for i, (n, at, _, cross, _, _, _) in enumerate(rings):
        partners[i, 0] = cross
        for kind in (0, 1):
            for _, jump in trees[i][kind]:
                for way in (jump, -jump):
                    partners[i, 1 + way % n] = at(way)
    partners[2, 0] = other_core
    rows_q, width = qf.shape
    rows_h, rows_g = 16 * nz, 16 * ny
    wh = width // 2

    def send(src, dst, ssem, rsem, to):
        copy = pltpu.make_async_remote_copy(
            src_ref=src, dst_ref=dst, send_sem=ssem, recv_sem=rsem, device_id=to, device_id_type=MESH
        )
        copy.start()
        return copy

    sent = []
    p_copy = pltpu.make_async_copy(p_hbm, pf, local_sem.at[0])
    p_copy.start()
    q_copy = pltpu.make_async_copy(q_hbm, qf, local_sem.at[1])
    q_copy.start()
    index_copies = [
        pltpu.make_async_copy(src, dst, local_sem.at[3 + i])
        for i, (src, dst) in enumerate(((pos_hbm, pos_ref), (owner_hbm, owner_ref), (row_hbm, row_ref)))
    ]
    for copy in index_copies:
        copy.start()
    barrier = pltpu.get_barrier_semaphore()
    for to in partners.values():
        pl.semaphore_signal(barrier, inc=1, device_id=to, device_id_type=MESH)
    p_copy.wait()
    mine = stacked(pf[...]).astype(BF16)
    hbuf[0, 0] = mine
    gbuf[0, 0] = mine
    pl.semaphore_wait(barrier, len(partners))

    arrive = [{}, {}]
    done = [{(0, 0)}, {(0, 0)}]

    def arrived(i, slot, kind):
        if (slot, kind) not in done[i]:
            arrive[i][(slot, kind)].wait_recv()
            done[i].add((slot, kind))

    def gather_sends(i, kind, pick):
        n, at, buf = rings[i][:3]
        for slot, jump in trees[i][kind]:
            if not pick(slot):
                continue
            src, dst = slot % n, (slot - jump) % n
            arrived(i, src, kind)
            arrive[i][(dst, kind)] = send(
                buf.at[src, kind], buf.at[dst, kind], ag_s.at[i, dst, kind], ag_r.at[i, dst, kind], at(jump)
            )

    for i, (n, at, buf, cross, _, _, _) in enumerate(rings):
        arrive[i][(0, 1)] = send(buf.at[0, 0], buf.at[0, 1], xa_s.at[i], xa_r.at[i], cross)
    for i in (0, 1):
        gather_sends(i, 0, lambda slot: slot == 0)

    q_copy.wait()
    q2[0:rows_q, :] = qf[...].astype(BF16)
    q_send = send(
        q2.at[pl.ds(0, rows_q)], q2.at[pl.ds(rows_q, rows_q)], core_s.at[0], core_r.at[0], other_core
    )
    shift_z, shift_y = max(nz // 2 - 2, 0), max(ny // 2 - 2, 0)
    negs = owner_ref.shape[0]
    for copy in index_copies:
        copy.wait()
    owner_t, row_t = owner_ref[...], row_ref[...]
    place = ((owner_t >> 1) - z + (nz + shift_z)) & (nz - 1)
    cross_bit = (owner_t >= 2 * nz).astype(I32) ^ xh
    column = place * 16 + cross_bit * 8 + row_t
    same_core = (owner_t & 1) == c
    codes[0, 0:negs, :] = jnp.where(same_core, column, -1)
    codes[1, 0:negs, :] = jnp.where(same_core, -1, column)
    codes[1, negs:8, :] = jnp.full((8 - negs, rows_q), -1, I32)
    code_send = send(codes.at[1], codes_in, core_s.at[1], core_r.at[1], other_core)
    sent += [q_send, code_send]
    row_ids = lax.broadcasted_iota(I32, (rows_h, rows_q), 0)

    def bias_of(code):
        named = row_ids == code[0:1, :]
        for k in range(1, negs):
            named = named | (row_ids == code[k : k + 1, :])
        return jnp.where(named, jnp.float32(0.0), jnp.float32(NONE))

    bias[:, 0:rows_q] = bias_of(codes[0, 0:negs, :])
    p = pos_ref[...]
    g_column = (((p >> 4) - y + (ny + shift_y)) & (ny - 1)) * 16 + (((p >> 3) & 1) ^ xl) * 8 + (p & 7)
    hit = lax.broadcasted_iota(I32, (rows_g, rows_q), 0) == g_column

    base = (0, rows_h)
    shifts = (shift_z, shift_y)

    def place_of(i, slot):
        return (slot + shifts[i]) % rings[i][0]

    def assemble(i, slot):
        buf = rings[i][2]
        for kind in (0, 1):
            arrived(i, slot, kind)
        first, second = buf[slot, 0].astype(F32), buf[slot, 1].astype(F32)
        at = base[i] + 16 * place_of(i, slot)
        bank[at : at + 16, 0:wh] = jnp.concatenate([first[0:8], second[0:8]], axis=0).astype(BF16)
        bank[at : at + 16, wh:width] = jnp.concatenate([first[8:16], second[8:16]], axis=0).astype(BF16)

    def scores(i, start, stop):
        if stop <= start:
            return
        rows = bank[base[i] + 16 * start : base[i] + 16 * stop, :]
        queries = q2[...] if i == 0 else q2[0:rows_q, :]
        out = lax.dot_general(rows, queries, (((1,), (1,)), ((), ())), preferred_element_type=F32) * SCALE
        if i == 0:
            sh[16 * start : 16 * stop, :] = out
        else:
            sg[16 * start : 16 * stop, :] = out

    for kind, least, most in ((1, 0, 0), (0, 1, 2), (1, 1, 2), (0, 3, 9)):
        for i in (0, 1):
            gather_sends(i, kind, lambda slot: least <= abs(slot) <= most)
    early = [max(2 * (ring[0] // 2 - 2) + 1, 0) for ring in rings]
    for i in (0, 1):
        for at in range(early[i]):
            assemble(i, (at - shifts[i]) % rings[i][0])
    q_send.wait_recv()
    for i in (0, 1):
        scores(i, 0, early[i])
    for i in (0, 1):
        gather_sends(i, 1, lambda slot: abs(slot) >= 3)
    code_send.wait_recv()
    bias[:, rows_q : 2 * rows_q] = bias_of(codes_in[...])
    for i in (0, 1):
        for at in range(early[i], rings[i][0]):
            assemble(i, (at - shifts[i]) % rings[i][0])
    for i in (0, 1):
        scores(i, early[i], rings[i][0])

    s_g = sg[...]
    s_h = sh[...] + bias[...]
    s_own, s_par = s_h[:, 0:rows_q], s_h[:, rows_q : 2 * rows_q]
    top_own = jnp.maximum(jnp.max(s_g, 0, keepdims=True), jnp.max(s_own, 0, keepdims=True))
    sum_own = jnp.sum(jnp.exp(s_g - top_own), 0, keepdims=True) + jnp.sum(
        jnp.exp(s_own - top_own), 0, keepdims=True
    )
    top_par = jnp.max(s_par, 0, keepdims=True)
    sum_par = jnp.sum(jnp.exp(s_par - top_par), 0, keepdims=True)
    lse_out[0:1, :] = top_own
    lse_out[1:2, :] = sum_own
    lse_out[2:3, :] = top_par
    lse_out[3:4, :] = sum_par
    lse_out[4:8, :] = jnp.zeros((4, rows_q), F32)
    lse_send = send(lse_out, lse_in, core_s.at[2], core_r.at[2], other_core)
    sent.append(lse_send)
    chosen = jnp.sum(jnp.where(hit, s_g, jnp.float32(0.0)), 0, keepdims=True)
    lse_send.wait_recv()

    def joined(top_a, sum_a, top_b, sum_b):
        top = jnp.maximum(top_a, top_b)
        return top + jnp.log(sum_a * jnp.exp(top_a - top) + sum_b * jnp.exp(top_b - top))

    lse = joined(top_own, sum_own, lse_in[2:3, :], lse_in[3:4, :])
    lse_par = joined(lse_in[0:1, :], lse_in[1:2, :], top_par, sum_par)
    loss_ref[...] = lse - chosen
    w_g = jnp.exp(s_g - lse) - hit.astype(F32)
    w_own = jnp.exp(s_own - lse)
    w_par = jnp.exp(s_par - lse_par)
    w_h = jnp.concatenate([w_own, w_par], axis=1).astype(BF16)
    w_gb = w_g.astype(BF16)

    def terms(i):
        weights, queries = (w_h, q2[...]) if i == 0 else (w_gb, q2[0:rows_q, :])
        rings[i][6][...] = jnp.dot(weights, queries, preferred_element_type=F32) * SCALE

    coming = [{}, {}]

    def summed(i, kind, slot):
        n, _, _, _, _, into, own = rings[i]
        at = 16 * place_of(i, slot % n) + 8 * kind
        value = stacked(own[at : at + 8, :])
        for e, copy in coming[i].get((kind, slot % n), []):
            copy.wait_recv()
            value = value + into[kind, e].astype(F32)
        return value

    def scatter_sends(i, kind, pick):
        n, at, _, _, out, into, _ = rings[i]
        edges = trees[i][kind]
        for e in range(len(edges) - 1, -1, -1):
            slot, jump = edges[e]
            if not pick(slot, slot - jump):
                continue
            out[kind, e] = summed(i, kind, slot - jump).astype(BF16)
            copy = send(out.at[kind, e], into.at[kind, e], rs_s.at[i, kind, e], rs_r.at[i, kind, e], at(-jump))
            coming[i].setdefault((kind, slot % n), []).append((e, copy))
            sent.append(copy)

    for i in (0, 1):
        terms(i)
        for kind in (1, 0):
            scatter_sends(i, kind, lambda slot, dst: abs(dst) == rings[i][0] // 2)
        for kind in (1, 0):
            sign = -1 if kind == 1 else 1
            scatter_sends(i, kind, lambda slot, dst: dst == 3 * sign and rings[i][0] > 6)
    for i in (0, 1):
        for kind in (1, 0):
            scatter_sends(i, kind, lambda slot, dst: abs(dst) == 1 and rings[i][0] > 2)
    w_par_q = jnp.transpose(w_par).astype(BF16)
    w_own_q = jnp.concatenate([jnp.transpose(w_own), jnp.transpose(w_g)], axis=1).astype(BF16)
    for h in (0, 1):
        cols = slice(h * wh, (h + 1) * wh)
        qs[:, cols] = (jnp.dot(w_par_q, bank[0:rows_h, cols], preferred_element_type=F32) * SCALE).astype(BF16)
    qg_send = send(qs, qr, core_s.at[3], core_r.at[3], other_core)
    sent.append(qg_send)
    for kind in (1, 0):
        sign = 1 if kind == 1 else -1
        for i in (0, 1):
            scatter_sends(i, kind, lambda slot, dst: dst == 3 * sign and rings[i][0] > 6)
    for h in (0, 1):
        cols = slice(h * wh, (h + 1) * wh)
        qf[:, cols] = jnp.dot(w_own_q, bank[:, cols], preferred_element_type=F32) * SCALE
    for kind in (1, 0):
        sign = -1 if kind == 1 else 1
        for i in (0, 1):
            scatter_sends(i, kind, lambda slot, dst: dst == 2 * sign and rings[i][0] > 4)
    qg_send.wait_recv()
    qg_ref[...] = qf[...] + qr[...].astype(F32)
    for kind in (1, 0):
        sign = 1 if kind == 1 else -1
        for i in (0, 1):
            scatter_sends(i, kind, lambda slot, dst: dst == 2 * sign and rings[i][0] > 4)

    crossing = []
    for i in (0, 1):
        xs[i] = summed(i, 1, 0).astype(BF16)
        crossing.append(send(xs.at[i], xr.at[i], xb_s.at[i], xb_r.at[i], rings[i][3]))
    sent += crossing
    total = summed(0, 0, 0) + summed(1, 0, 0)
    for i in (0, 1):
        crossing[i].wait_recv()
        total = total + xr[i].astype(F32)
    pg_ref[:, 0:wh] = total[0:8]
    pg_ref[:, wh:width] = total[8:16]
    for i in (0, 1):
        for copy in arrive[i].values():
            copy.wait_send()
    for copy in sent:
        copy.wait_send()


def hand_over(*refs):
    count = len(refs) // 2
    sem = refs[-1]
    copies = [pltpu.make_async_copy(refs[i], refs[count + i], sem.at[i]) for i in range(count)]
    for copy in copies:
        copy.start()
    for copy in copies:
        copy.wait()


def body(queries, passages, positive, neg_owner, neg_row):
    nblk, nshard = lax.axis_size("blk"), lax.axis_size("shard")
    ny, nz = nblk // 2, nshard // 4
    rows_q, width = queries.shape
    rows_p = passages.shape[0]
    negs = neg_owner.shape[1]
    wh = width // 2
    vmem = pl.BlockSpec(memory_space=pltpu.VMEM)
    anywhere = pl.BlockSpec(memory_space=pl.ANY)
    hbm = pl.BlockSpec(memory_space=pltpu.HBM)
    dma = pltpu.SemaphoreType.DMA
    top = max(ny, nz)
    scratch = [
        pltpu.VMEM((rows_q, width), F32),
        pltpu.VMEM((rows_p, width), F32),
        pltpu.VMEM((1, rows_q), I32),
        pltpu.VMEM((negs, rows_q), I32),
        pltpu.VMEM((negs, rows_q), I32),
        pltpu.VMEM((2 * rows_q, width), BF16),
        pltpu.VMEM((nz, 2, 16, wh), BF16),
        pltpu.VMEM((ny, 2, 16, wh), BF16),
        pltpu.VMEM((16 * (nz + ny), width), BF16),
        pltpu.VMEM((16 * nz, 2 * rows_q), F32),
        pltpu.VMEM((16 * ny, rows_q), F32),
        pltpu.VMEM((16 * nz, 2 * rows_q), F32),
        pltpu.VMEM((2, 8, rows_q), I32),
        pltpu.VMEM((8, rows_q), I32),
        pltpu.VMEM((8, rows_q), F32),
        pltpu.VMEM((8, rows_q), F32),
        pltpu.VMEM((16 * nz, width), F32),
        pltpu.VMEM((16 * ny, width), F32),
        pltpu.VMEM((2, nz - 1, 16, wh), BF16),
        pltpu.VMEM((2, nz - 1, 16, wh), BF16),
        pltpu.VMEM((2, ny - 1, 16, wh), BF16),
        pltpu.VMEM((2, ny - 1, 16, wh), BF16),
        pltpu.VMEM((2, 16, wh), BF16),
        pltpu.VMEM((2, 16, wh), BF16),
        pltpu.VMEM((rows_q, width), BF16),
        pltpu.VMEM((rows_q, width), BF16),
        dma((6,)),
        dma((2, top, 2)), dma((2, top, 2)),
        dma((2,)), dma((2,)),
        dma((4,)), dma((4,)),
        dma((2, 2, top - 1)), dma((2, 2, top - 1)),
        dma((2,)), dma((2,)),
    ]
    inputs = (queries, passages, positive.reshape(1, rows_q), neg_owner.T, neg_row.T)
    qg, pg, loss = pl.pallas_call(
        functools.partial(kernel, nblk, nshard),
        out_shape=(
            pltpu.VMEM((rows_q, width), F32),
            pltpu.VMEM((rows_p, width), F32),
            pltpu.VMEM((1, rows_q), F32),
        ),
        in_specs=[hbm] * 5,
        out_specs=(vmem,) * 3,
        scratch_shapes=scratch,
        compiler_params=pltpu.CompilerParams(
            collective_id=0, has_side_effects=True, vmem_limit_bytes=40 * 1024 * 1024
        ),
    )(*[pltpu.with_memory_space_constraint(a, pltpu.HBM) for a in inputs])
    qg, pg, loss = pl.pallas_call(
        hand_over,
        out_shape=tuple(jax.ShapeDtypeStruct(a.shape, a.dtype) for a in (qg, pg, loss)),
        in_specs=[anywhere] * 3,
        out_specs=(hbm,) * 3,
        scratch_shapes=[dma((3,))],
    )(*[pltpu.with_memory_space_constraint(a, pltpu.VMEM) for a in (qg, pg, loss)])
    return (qg, pg, loss.reshape(rows_q))


def solution(mesh):
    rows = P(("blk", "shard"), None)
    flat = P(("blk", "shard"))
    return jax.shard_map(
        body,
        mesh=mesh,
        in_specs=(rows, rows, flat, rows, rows),
        out_specs=(rows, rows, flat),
        check_vma=False,
    )
```

time: 62.3 us -> 54.9 us (0.88); the launches traced: 61.5 us -> 54.8 us
  local copies, waits for them, and re-layouts: 6.81 us -> 0 us
    unnamed x13 -> x0, local copies, waits for them, and re-layouts: 6.81 us -> none
    pallas_call x1 -> x2, Pallas kernels: 54.1 us -> 54.1 us  [the longest x1 52.9 us: body(): pl.pallas_call(functools.partial(kernel, nblk, nshard), out_shape=(pltpu....]
where the time goes in v3:
time: 54.9 us; the launch traced here: 54.8 us
  Pallas kernels  54.1 us (99%)
  between operations  0.64 us (1%)
    pallas_call x1, Pallas kernels, body(): pl.pallas_call(functools.partial(kernel, nblk, nshard), out_shape=(pltpu....  52.9 us
    pallas_call x1, Pallas kernels, body(): pl.pallas_call(hand_over, out_shape=tuple((jax.ShapeDtypeStruct(a.shape,...  1.28 us

profile of v3, /device:TPU:1, one launch (start us, length us, event | category | flops | bytes accessed | tf_op | source)
XLA Modules:
  0.0 54.8 jit_solution(897777142206606945)
XLA Ops:
  0.6 52.9 %shard_map.76 = (f32[128,3584]{1,0:T(8,128)S(1)}, f32[8,3584]{1,0:T(8,128)S(1)}, f32[1,128]{1,0:T(1,128)S(1)}) custom-call(f32[128,3584]{1,0:T(8,128)} %q_hbm.1, f32[8,3584]{1,0:T(8,128)} %p_hbm.1, s32[1,128]{1,0:T(1,128)} %bitcast.6, s32[7,128]{1,0:T(8,128)} %bitcast.4, s32[7,128]{1,0:T(8,128)} %bitcast.5), custom_call_target="tpu_custom_call" | custom-call | tf_op jit(solution)/shard_map/pallas_call | solution.py:374
  53.5 1.3 %shard_map.77 = (f32[128,3584]{1,0:T(8,128)}, f32[8,3584]{1,0:T(8,128)}, f32[1,128]{1,0:T(1,128)}) custom-call(f32[128,3584]{1,0:T(8,128)S(1)} %get-tuple-element.9.refs_0_, f32[8,3584]{1,0:T(8,128)S(1)} %get-tuple-element.10.refs_1_, f32[1,128]{1,0:T(1,128)S(1)} %get-tuple-element.11.refs_2_), custom_call_target="tpu_custom_call" | custom-call | tf_op jit(solution)/shard_map/pallas_call | solution.py:388

commit v4 on v3

--- a/solution.py
+++ b/solution.py
@@ -18,17 +18,46 @@
     return jnp.concatenate([wide[:, :half], wide[:, half:]], axis=0)
 
 
-def tree(n, kind):
-    half = n // 2
-    direct = 2 if half > 2 else 1
-    edges = []
-    for d in range(direct, 0, -1):
-        if d < half:
-            edges += [(0, d), (0, -d)]
-    for d in range(direct + 1, half):
-        edges += [(1 - d, 1), (d - 1, -1)]
-    edges.append((1 - half, 1) if kind == 0 else (half - 1, -1))
-    return edges
+GATHER = (
+    ((0, -2), (0, 0), 0, 2),
+    ((0, 2), (0, 0), 0, -2),
+    ((0, 1), (0, 0), 0, -1),
+    ((1, 0), (0, 0), 1, 0),
+    ((1, -1), (1, 0), 0, 1),
+    ((1, 2), (1, 0), 0, -2),
+    ((1, -2), (0, -2), 1, 0),
+    ((0, -1), (0, -2), 0, -1),
+    ((0, -3), (0, -2), 0, 1),
+    ((0, 3), (0, 2), 0, -1),
+    ((1, 1), (1, 0), 0, -1),
+    ((0, 4), (0, -2), 0, 2),
+    ((1, 4), (1, -2), 0, 2),
+    ((1, -3), (0, -3), 1, 0),
+    ((1, 3), (1, 2), 0, -1),
+)
+SCATTER = (
+    ((1, 4), (0, 4), 1, 0),
+    ((1, -3), (1, -2), 0, 1),
+    ((1, 3), (1, 2), 0, -1),
+    ((1, -1), (0, -1), 1, 0),
+    ((0, 3), (0, 2), 0, -1),
+    ((0, 1), (0, 2), 0, 1),
+    ((1, 1), (1, 0), 0, -1),
+    ((0, -3), (0, -2), 0, 1),
+    ((0, 4), (0, -2), 0, 2),
+    ((1, -2), (0, -2), 1, 0),
+    ((1, 2), (1, 0), 0, -2),
+    ((0, -1), (0, 0), 0, 1),
+    ((0, 2), (0, 0), 0, -2),
+    ((0, -2), (0, 0), 0, 2),
+    ((1, 0), (0, 0), 1, 0),
+)
+PAIR = (((0, 1), (0, 0), 0, -1), ((1, 0), (0, 0), 1, 0), ((1, 1), (1, 0), 0, -1))
+
+
+def table(n, scatter):
+    rows = (SCATTER if scatter else GATHER) if n == 8 else (PAIR[::-1] if scatter else PAIR)
+    return [((k, r % n), (pk, pr % n), cross, jump) for (k, r), (pk, pr), cross, jump in rows]
 
 
 def kernel(
@@ -36,8 +65,8 @@
     q_hbm, p_hbm, pos_hbm, owner_hbm, row_hbm,
     qg_ref, pg_ref, loss_ref,
     qf, pf, pos_ref, owner_ref, row_ref, q2, hbuf, gbuf, bank, sh, sg, bias, codes, codes_in, lse_out, lse_in,
-    part_h, part_g, hs, hr, gs, gr, xs, xr, qs, qr,
-    local_sem, ag_s, ag_r, xa_s, xa_r, core_s, core_r, rs_s, rs_r, xb_s, xb_r,
+    part_h, part_g, hs, hr, gs, gr, qs, qr,
+    local_sem, ag_s, ag_r, core_s, core_r, rs_s, rs_r,
 ):
     ny, nz = nblk // 2, nshard // 4
     b, s = lax.axis_index("blk"), lax.axis_index("shard")
@@ -47,28 +76,23 @@
     def device(y_, xl_, xh_, z_, c_):
         return (y_ * 2 + xl_, xh_ * (2 * nz) + z_ * 2 + c_)
 
-    def along_z(jump):
-        return device(y, xl, xh, lax.rem(z + (jump + nz), nz), c)
-
-    def along_y(jump):
-        return device(lax.rem(y + (jump + ny), ny), xl, xh, z, c)
-
-    other_xh = device(y, xl, 1 - xh, z, c)
-    other_xl = device(y, 1 - xl, xh, z, c)
+    def along_z(cross, jump):
+        return device(y, xl, 1 - xh if cross else xh, lax.rem(z + (jump + nz), nz), c)
+
+    def along_y(cross, jump):
+        return device(lax.rem(y + (jump + ny), ny), 1 - xl if cross else xl, xh, z, c)
+
     other_core = device(y, xl, xh, z, 1 - c)
     rings = (
-        (nz, along_z, hbuf, other_xh, hs, hr, part_h),
-        (ny, along_y, gbuf, other_xl, gs, gr, part_g),
+        (nz, along_z, hbuf, hs, hr, part_h, table(nz, False), table(nz, True)),
+        (ny, along_y, gbuf, gs, gr, part_g, table(ny, False), table(ny, True)),
     )
-    trees = [[tree(ring[0], kind) for kind in (0, 1)] for ring in rings]
-    partners = {}
-    for i, (n, at, _, cross, _, _, _) in enumerate(rings):
-        partners[i, 0] = cross
-        for kind in (0, 1):
-            for _, jump in trees[i][kind]:
+    partners = {(2, 0, 0): other_core}
+    for i, ring in enumerate(rings):
+        for rows in ring[6:8]:
+            for _, _, cross, jump in rows:
                 for way in (jump, -jump):
-                    partners[i, 1 + way % n] = at(way)
-    partners[2, 0] = other_core
+                    partners[i, cross, way % ring[0]] = ring[1](cross, way)
     rows_q, width = qf.shape
     rows_h, rows_g = 16 * nz, 16 * ny
     wh = width // 2
@@ -103,26 +127,28 @@
     arrive = [{}, {}]
     done = [{(0, 0)}, {(0, 0)}]
 
-    def arrived(i, slot, kind):
-        if (slot, kind) not in done[i]:
-            arrive[i][(slot, kind)].wait_recv()
-            done[i].add((slot, kind))
-
-    def gather_sends(i, kind, pick):
-        n, at, buf = rings[i][:3]
-        for slot, jump in trees[i][kind]:
-            if not pick(slot):
-                continue
-            src, dst = slot % n, (slot - jump) % n
-            arrived(i, src, kind)
-            arrive[i][(dst, kind)] = send(
-                buf.at[src, kind], buf.at[dst, kind], ag_s.at[i, dst, kind], ag_r.at[i, dst, kind], at(jump)
-            )
-
-    for i, (n, at, buf, cross, _, _, _) in enumerate(rings):
-        arrive[i][(0, 1)] = send(buf.at[0, 0], buf.at[0, 1], xa_s.at[i], xa_r.at[i], cross)
-    for i in (0, 1):
-        gather_sends(i, 0, lambda slot: slot == 0)
+    def arrived(i, node):
+        if node not in done[i]:
+            arrive[i][node].wait_recv()
+            done[i].add(node)
+
+    def gather_sends(start, stop):
+        for e in range(start, stop):
+            for i, ring in enumerate(rings):
+                at, buf, rows = ring[1], ring[2], ring[6]
+                if e >= len(rows):
+                    continue
+                (kind, slot), (from_kind, from_slot), cross, jump = rows[e]
+                arrived(i, (from_kind, from_slot))
+                arrive[i][kind, slot] = send(
+                    buf.at[from_slot, from_kind],
+                    buf.at[slot, kind],
+                    ag_s.at[i, e],
+                    ag_r.at[i, e],
+                    at(cross, jump),
+                )
+
+    gather_sends(0, 4 if nz == 8 or ny == 8 else 2)
 
     q_copy.wait()
     q2[0:rows_q, :] = qf[...].astype(BF16)
@@ -165,7 +191,7 @@
     def assemble(i, slot):
         buf = rings[i][2]
         for kind in (0, 1):
-            arrived(i, slot, kind)
+            arrived(i, (kind, slot))
         first, second = buf[slot, 0].astype(F32), buf[slot, 1].astype(F32)
         at = base[i] + 16 * place_of(i, slot)
         bank[at : at + 16, 0:wh] = jnp.concatenate([first[0:8], second[0:8]], axis=0).astype(BF16)
@@ -182,18 +208,14 @@
         else:
             sg[16 * start : 16 * stop, :] = out
 
-    for kind, least, most in ((1, 0, 0), (0, 1, 2), (1, 1, 2), (0, 3, 9)):
-        for i in (0, 1):
-            gather_sends(i, kind, lambda slot: least <= abs(slot) <= most)
-    early = [max(2 * (ring[0] // 2 - 2) + 1, 0) for ring in rings]
+    gather_sends(4 if nz == 8 or ny == 8 else 2, 15)
+    early = [3 if ring[0] == 8 else 0 for ring in rings]
     for i in (0, 1):
         for at in range(early[i]):
             assemble(i, (at - shifts[i]) % rings[i][0])
     q_send.wait_recv()
     for i in (0, 1):
         scores(i, 0, early[i])
-    for i in (0, 1):
-        gather_sends(i, 1, lambda slot: abs(slot) >= 3)
     code_send.wait_recv()
     bias[:, rows_q : 2 * rows_q] = bias_of(codes_in[...])
     for i in (0, 1):
@@ -236,41 +258,40 @@
 
     def terms(i):
         weights, queries = (w_h, q2[...]) if i == 0 else (w_gb, q2[0:rows_q, :])
-        rings[i][6][...] = jnp.dot(weights, queries, preferred_element_type=F32) * SCALE
+        rings[i][5][...] = jnp.dot(weights, queries, preferred_element_type=F32) * SCALE
 
     coming = [{}, {}]
 
-    def summed(i, kind, slot):
-        n, _, _, _, _, into, own = rings[i]
-        at = 16 * place_of(i, slot % n) + 8 * kind
+    def summed(i, node):
+        kind, slot = node
+        into, own = rings[i][4:6]
+        at = 16 * place_of(i, slot) + 8 * kind
         value = stacked(own[at : at + 8, :])
-        for e, copy in coming[i].get((kind, slot % n), []):
+        for e, copy in coming[i].get(node, []):
             copy.wait_recv()
-            value = value + into[kind, e].astype(F32)
+            value = value + into[e].astype(F32)
         return value
 
-    def scatter_sends(i, kind, pick):
-        n, at, _, _, out, into, _ = rings[i]
-        edges = trees[i][kind]
-        for e in range(len(edges) - 1, -1, -1):
-            slot, jump = edges[e]
-            if not pick(slot, slot - jump):
-                continue
-            out[kind, e] = summed(i, kind, slot - jump).astype(BF16)
-            copy = send(out.at[kind, e], into.at[kind, e], rs_s.at[i, kind, e], rs_r.at[i, kind, e], at(-jump))
-            coming[i].setdefault((kind, slot % n), []).append((e, copy))
-            sent.append(copy)
-
+    def scatter_send(i, e):
+        at, out, into, rows = rings[i][1], rings[i][3], rings[i][4], rings[i][7]
+        if e >= len(rows):
+            return
+        node, parent, cross, jump = rows[e]
+        out[e] = summed(i, node).astype(BF16)
+        copy = send(out.at[e], into.at[e], rs_s.at[i, e], rs_r.at[i, e], at(cross, -jump))
+        coming[i].setdefault(parent, []).append((e, copy))
+        sent.append(copy)
+
+    def scatter_sends(start, stop):
+        for e in range(start, stop):
+            for i in (0, 1):
+                scatter_send(i, e)
+
+    leaves = 8 if nz == 8 or ny == 8 else 1
     for i in (0, 1):
         terms(i)
-        for kind in (1, 0):
-            scatter_sends(i, kind, lambda slot, dst: abs(dst) == rings[i][0] // 2)
-        for kind in (1, 0):
-            sign = -1 if kind == 1 else 1
-            scatter_sends(i, kind, lambda slot, dst: dst == 3 * sign and rings[i][0] > 6)
-    for i in (0, 1):
-        for kind in (1, 0):
-            scatter_sends(i, kind, lambda slot, dst: abs(dst) == 1 and rings[i][0] > 2)
+        for e in range(leaves):
+            scatter_send(i, e)
     w_par_q = jnp.transpose(w_par).astype(BF16)
     w_own_q = jnp.concatenate([jnp.transpose(w_own), jnp.transpose(w_g)], axis=1).astype(BF16)
     for h in (0, 1):
@@ -278,33 +299,15 @@
         qs[:, cols] = (jnp.dot(w_par_q, bank[0:rows_h, cols], preferred_element_type=F32) * SCALE).astype(BF16)
     qg_send = send(qs, qr, core_s.at[3], core_r.at[3], other_core)
     sent.append(qg_send)
-    for kind in (1, 0):
-        sign = 1 if kind == 1 else -1
-        for i in (0, 1):
-            scatter_sends(i, kind, lambda slot, dst: dst == 3 * sign and rings[i][0] > 6)
+    scatter_sends(leaves, 10)
     for h in (0, 1):
         cols = slice(h * wh, (h + 1) * wh)
         qf[:, cols] = jnp.dot(w_own_q, bank[:, cols], preferred_element_type=F32) * SCALE
-    for kind in (1, 0):
-        sign = -1 if kind == 1 else 1
-        for i in (0, 1):
-            scatter_sends(i, kind, lambda slot, dst: dst == 2 * sign and rings[i][0] > 4)
+    scatter_sends(10, 13)
     qg_send.wait_recv()
     qg_ref[...] = qf[...] + qr[...].astype(F32)
-    for kind in (1, 0):
-        sign = 1 if kind == 1 else -1
-        for i in (0, 1):
-            scatter_sends(i, kind, lambda slot, dst: dst == 2 * sign and rings[i][0] > 4)
-
-    crossing = []
-    for i in (0, 1):
-        xs[i] = summed(i, 1, 0).astype(BF16)
-        crossing.append(send(xs.at[i], xr.at[i], xb_s.at[i], xb_r.at[i], rings[i][3]))
-    sent += crossing
-    total = summed(0, 0, 0) + summed(1, 0, 0)
-    for i in (0, 1):
-        crossing[i].wait_recv()
-        total = total + xr[i].astype(F32)
+    scatter_sends(13, 15)
+    total = summed(0, (0, 0)) + summed(1, (0, 0))
     pg_ref[:, 0:wh] = total[0:8]
     pg_ref[:, wh:width] = total[8:16]
     for i in (0, 1):
@@ -355,20 +358,16 @@
         pltpu.VMEM((8, rows_q), F32),
         pltpu.VMEM((16 * nz, width), F32),
         pltpu.VMEM((16 * ny, width), F32),
-        pltpu.VMEM((2, nz - 1, 16, wh), BF16),
-        pltpu.VMEM((2, nz - 1, 16, wh), BF16),
-        pltpu.VMEM((2, ny - 1, 16, wh), BF16),
-        pltpu.VMEM((2, ny - 1, 16, wh), BF16),
-        pltpu.VMEM((2, 16, wh), BF16),
-        pltpu.VMEM((2, 16, wh), BF16),
+        pltpu.VMEM((2 * nz - 1, 16, wh), BF16),
+        pltpu.VMEM((2 * nz - 1, 16, wh), BF16),
+        pltpu.VMEM((2 * ny - 1, 16, wh), BF16),
+        pltpu.VMEM((2 * ny - 1, 16, wh), BF16),
         pltpu.VMEM((rows_q, width), BF16),
         pltpu.VMEM((rows_q, width), BF16),
         dma((6,)),
-        dma((2, top, 2)), dma((2, top, 2)),
-        dma((2,)), dma((2,)),
+        dma((2, 2 * top - 1)), dma((2, 2 * top - 1)),
         dma((4,)), dma((4,)),
-        dma((2, 2, top - 1)), dma((2, 2, top - 1)),
-        dma((2,)), dma((2,)),
+        dma((2, 2 * top - 1)), dma((2, 2 * top - 1)),
     ]
     inputs = (queries, passages, positive.reshape(1, rows_q), neg_owner.T, neg_row.T)
     qg, pg, loss = pl.pallas_call(

time: 54.9 us -> 51.2 us (0.933)
  Pallas kernels: 54.1 us -> 50.5 us
    pallas_call x1, Pallas kernels: 52.9 us -> 49.2 us  [body(): pl.pallas_call(functools.partial(kernel, nblk, nshard), out_shape=(pltpu....]
where the time goes in v4:
time: 51.2 us; the launch traced here: 51.1 us
  Pallas kernels  50.5 us (99%)
  between operations  0.64 us (1%)
    pallas_call x1, Pallas kernels, body(): pl.pallas_call(functools.partial(kernel, nblk, nshard), out_shape=(pltpu....  49.2 us
    pallas_call x1, Pallas kernels, body(): pl.pallas_call(hand_over, out_shape=tuple((jax.ShapeDtypeStruct(a.shape,...  1.28 us

profile of v4, /device:TPU:1, one launch (start us, length us, event | category | flops | bytes accessed | tf_op | source)
XLA Modules:
  0.0 51.1 jit_solution(573227342183744853)
XLA Ops:
  0.6 49.2 %shard_map.76 = (f32[128,3584]{1,0:T(8,128)S(1)}, f32[8,3584]{1,0:T(8,128)S(1)}, f32[1,128]{1,0:T(1,128)S(1)}) custom-call(f32[128,3584]{1,0:T(8,128)} %q_hbm.1, f32[8,3584]{1,0:T(8,128)} %p_hbm.1, s32[1,128]{1,0:T(1,128)} %bitcast.6, s32[7,128]{1,0:T(8,128)} %bitcast.4, s32[7,128]{1,0:T(8,128)} %bitcast.5), custom_call_target="tpu_custom_call" | custom-call | tf_op jit(solution)/shard_map/pallas_call | solution.py:373
  49.8 1.3 %shard_map.77 = (f32[128,3584]{1,0:T(8,128)}, f32[8,3584]{1,0:T(8,128)}, f32[1,128]{1,0:T(1,128)}) custom-call(f32[128,3584]{1,0:T(8,128)S(1)} %get-tuple-element.9.refs_0_, f32[8,3584]{1,0:T(8,128)S(1)} %get-tuple-element.10.refs_1_, f32[1,128]{1,0:T(1,128)S(1)} %get-tuple-element.11.refs_2_), custom_call_target="tpu_custom_call" | custom-call | tf_op jit(solution)/shard_map/pallas_call | solution.py:387

commit v5 on v4

--- a/solution.py
+++ b/solution.py
@@ -19,39 +19,40 @@
 
 
 GATHER = (
-    ((0, -2), (0, 0), 0, 2),
-    ((0, 2), (0, 0), 0, -2),
-    ((0, 1), (0, 0), 0, -1),
-    ((1, 0), (0, 0), 1, 0),
-    ((1, -1), (1, 0), 0, 1),
-    ((1, 2), (1, 0), 0, -2),
-    ((1, -2), (0, -2), 1, 0),
-    ((0, -1), (0, -2), 0, -1),
-    ((0, -3), (0, -2), 0, 1),
-    ((0, 3), (0, 2), 0, -1),
-    ((1, 1), (1, 0), 0, -1),
-    ((0, 4), (0, -2), 0, 2),
-    ((1, 4), (1, -2), 0, 2),
-    ((1, -3), (0, -3), 1, 0),
-    ((1, 3), (1, 2), 0, -1),
-)
-SCATTER = (
-    ((1, 4), (0, 4), 1, 0),
-    ((1, -3), (1, -2), 0, 1),
-    ((1, 3), (1, 2), 0, -1),
-    ((1, -1), (0, -1), 1, 0),
-    ((0, 3), (0, 2), 0, -1),
-    ((0, 1), (0, 2), 0, 1),
-    ((1, 1), (1, 0), 0, -1),
-    ((0, -3), (0, -2), 0, 1),
-    ((0, 4), (0, -2), 0, 2),
-    ((1, -2), (0, -2), 1, 0),
-    ((1, 2), (1, 0), 0, -2),
-    ((0, -1), (0, 0), 0, 1),
     ((0, 2), (0, 0), 0, -2),
     ((0, -2), (0, 0), 0, 2),
     ((1, 0), (0, 0), 1, 0),
+    ((1, 2), (0, 2), 1, 0),
+    ((0, 4), (0, 2), 0, -2),
+    ((0, -3), (0, -2), 0, 1),
+    ((1, -1), (1, 0), 0, 1),
+    ((0, 1), (0, 2), 0, 1),
+    ((1, 1), (1, 0), 0, -1),
+    ((1, -2), (0, -2), 1, 0),
+    ((0, -1), (0, 0), 0, 1),
+    ((1, 3), (1, 2), 0, -1),
+    ((1, 4), (1, 2), 0, -2),
+    ((1, -3), (0, -3), 1, 0),
+    ((0, 3), (0, 4), 0, 1),
 )
+SCATTER = (
+    ((1, 3), (1, 2), 0, -1),
+    ((1, 4), (0, 4), 1, 0),
+    ((1, -3), (1, -2), 0, 1),
+    ((1, 1), (0, 1), 1, 0),
+    ((0, 3), (0, 1), 0, -2),
+    ((0, -3), (0, -2), 0, 1),
+    ((1, -1), (1, 0), 0, 1),
+    ((0, 4), (0, 2), 0, -2),
+    ((1, -2), (1, 0), 0, 2),
+    ((1, 2), (0, 2), 1, 0),
+    ((0, 1), (0, 0), 0, -1),
+    ((0, -2), (0, 0), 0, 2),
+    ((0, -1), (0, 0), 0, 1),
+    ((0, 2), (0, 0), 0, -2),
+    ((1, 0), (0, 0), 1, 0),
+)
+FIRST, LEAVES = 3, 7
 PAIR = (((0, 1), (0, 0), 0, -1), ((1, 0), (0, 0), 1, 0), ((1, 1), (1, 0), 0, -1))
 
 
@@ -64,8 +65,8 @@
     nblk, nshard,
     q_hbm, p_hbm, pos_hbm, owner_hbm, row_hbm,
     qg_ref, pg_ref, loss_ref,
-    qf, pf, pos_ref, owner_ref, row_ref, q2, hbuf, gbuf, bank, sh, sg, bias, codes, codes_in, lse_out, lse_in,
-    part_h, part_g, hs, hr, gs, gr, qs, qr,
+    qf, pf, pos_ref, owner_ref, row_ref, q2, hbuf, gbuf, bank, q2t, sc, bias, codes, codes_in, lse_out, lse_in,
+    part, hs, hr, gs, gr, qs, qr,
     local_sem, ag_s, ag_r, core_s, core_r, rs_s, rs_r,
 ):
     ny, nz = nblk // 2, nshard // 4
@@ -84,12 +85,12 @@
 
     other_core = device(y, xl, xh, z, 1 - c)
     rings = (
-        (nz, along_z, hbuf, hs, hr, part_h, table(nz, False), table(nz, True)),
-        (ny, along_y, gbuf, gs, gr, part_g, table(ny, False), table(ny, True)),
+        (nz, along_z, hbuf, hs, hr, table(nz, False), table(nz, True)),
+        (ny, along_y, gbuf, gs, gr, table(ny, False), table(ny, True)),
     )
     partners = {(2, 0, 0): other_core}
     for i, ring in enumerate(rings):
-        for rows in ring[6:8]:
+        for rows in ring[5:7]:
             for _, _, cross, jump in rows:
                 for way in (jump, -jump):
                     partners[i, cross, way % ring[0]] = ring[1](cross, way)
@@ -135,7 +136,7 @@
     def gather_sends(start, stop):
         for e in range(start, stop):
             for i, ring in enumerate(rings):
-                at, buf, rows = ring[1], ring[2], ring[6]
+                at, buf, rows = ring[1], ring[2], ring[5]
                 if e >= len(rows):
                     continue
                 (kind, slot), (from_kind, from_slot), cross, jump = rows[e]
@@ -148,13 +149,15 @@
                     at(cross, jump),
                 )
 
-    gather_sends(0, 4 if nz == 8 or ny == 8 else 2)
+    first = FIRST if nz == 8 or ny == 8 else 2
+    gather_sends(0, first)
 
     q_copy.wait()
     q2[0:rows_q, :] = qf[...].astype(BF16)
     q_send = send(
         q2.at[pl.ds(0, rows_q)], q2.at[pl.ds(rows_q, rows_q)], core_s.at[0], core_r.at[0], other_core
     )
+    q2t[:, 0:rows_q] = jnp.transpose(q2[0:rows_q, :])
     shift_z, shift_y = max(nz // 2 - 2, 0), max(ny // 2 - 2, 0)
     negs = owner_ref.shape[0]
     for copy in index_copies:
@@ -182,8 +185,13 @@
     g_column = (((p >> 4) - y + (ny + shift_y)) & (ny - 1)) * 16 + (((p >> 3) & 1) ^ xl) * 8 + (p & 7)
     hit = lax.broadcasted_iota(I32, (rows_g, rows_q), 0) == g_column
 
-    base = (0, rows_h)
     shifts = (shift_z, shift_y)
+    early = [3 if ring[0] == 8 else 0 for ring in rings]
+    first_late = 16 * (early[0] + early[1])
+    starts = ((0, first_late), (16 * early[0], first_late + 16 * (nz - early[0])))
+
+    def row_of(i, place):
+        return starts[i][0] + 16 * place if place < early[i] else starts[i][1] + 16 * (place - early[i])
 
     def place_of(i, slot):
         return (slot + shifts[i]) % rings[i][0]
@@ -193,39 +201,35 @@
         for kind in (0, 1):
             arrived(i, (kind, slot))
         first, second = buf[slot, 0].astype(F32), buf[slot, 1].astype(F32)
-        at = base[i] + 16 * place_of(i, slot)
+        at = row_of(i, place_of(i, slot))
         bank[at : at + 16, 0:wh] = jnp.concatenate([first[0:8], second[0:8]], axis=0).astype(BF16)
         bank[at : at + 16, wh:width] = jnp.concatenate([first[8:16], second[8:16]], axis=0).astype(BF16)
 
-    def scores(i, start, stop):
-        if stop <= start:
-            return
-        rows = bank[base[i] + 16 * start : base[i] + 16 * stop, :]
-        queries = q2[...] if i == 0 else q2[0:rows_q, :]
-        out = lax.dot_general(rows, queries, (((1,), (1,)), ((), ())), preferred_element_type=F32) * SCALE
-        if i == 0:
-            sh[16 * start : 16 * stop, :] = out
-        else:
-            sg[16 * start : 16 * stop, :] = out
-
-    gather_sends(4 if nz == 8 or ny == 8 else 2, 15)
-    early = [3 if ring[0] == 8 else 0 for ring in rings]
+    def scores(start, stop):
+        if stop > start:
+            sc[start:stop, :] = jnp.dot(bank[start:stop, :], q2t[...], preferred_element_type=F32) * SCALE
+
+    gather_sends(first, 15)
+    q_send.wait_recv()
+    q2t[:, rows_q : 2 * rows_q] = jnp.transpose(q2[rows_q : 2 * rows_q, :])
     for i in (0, 1):
         for at in range(early[i]):
             assemble(i, (at - shifts[i]) % rings[i][0])
-    q_send.wait_recv()
-    for i in (0, 1):
-        scores(i, 0, early[i])
+    scores(0, first_late)
     code_send.wait_recv()
     bias[:, rows_q : 2 * rows_q] = bias_of(codes_in[...])
     for i in (0, 1):
         for at in range(early[i], rings[i][0]):
             assemble(i, (at - shifts[i]) % rings[i][0])
-    for i in (0, 1):
-        scores(i, early[i], rings[i][0])
-
-    s_g = sg[...]
-    s_h = sh[...] + bias[...]
+    scores(first_late, rows_h + rows_g)
+
+    def ring_rows(ref, i, cols):
+        parts = [ref[starts[i][0] : starts[i][0] + 16 * early[i], cols]] if early[i] else []
+        late = starts[i][1]
+        return jnp.concatenate(parts + [ref[late : late + 16 * (rings[i][0] - early[i]), cols]], axis=0)
+
+    s_g = ring_rows(sc, 1, slice(0, rows_q))
+    s_h = ring_rows(sc, 0, slice(0, 2 * rows_q)) + bias[...]
     s_own, s_par = s_h[:, 0:rows_q], s_h[:, rows_q : 2 * rows_q]
     top_own = jnp.maximum(jnp.max(s_g, 0, keepdims=True), jnp.max(s_own, 0, keepdims=True))
     sum_own = jnp.sum(jnp.exp(s_g - top_own), 0, keepdims=True) + jnp.sum(
@@ -253,27 +257,30 @@
     w_g = jnp.exp(s_g - lse) - hit.astype(F32)
     w_own = jnp.exp(s_own - lse)
     w_par = jnp.exp(s_par - lse_par)
-    w_h = jnp.concatenate([w_own, w_par], axis=1).astype(BF16)
-    w_gb = w_g.astype(BF16)
-
-    def terms(i):
-        weights, queries = (w_h, q2[...]) if i == 0 else (w_gb, q2[0:rows_q, :])
-        rings[i][5][...] = jnp.dot(weights, queries, preferred_element_type=F32) * SCALE
+    w_all = jnp.concatenate(
+        [
+            jnp.concatenate([w_own, w_par], axis=1),
+            jnp.concatenate([w_g, jnp.zeros((rows_g, rows_q), F32)], axis=1),
+        ],
+        axis=0,
+    ).astype(BF16)
+
+    part[...] = jnp.dot(w_all, q2[...], preferred_element_type=F32) * SCALE
 
     coming = [{}, {}]
 
     def summed(i, node):
         kind, slot = node
-        into, own = rings[i][4:6]
-        at = 16 * place_of(i, slot) + 8 * kind
-        value = stacked(own[at : at + 8, :])
+        into = rings[i][4]
+        at = i * rows_h + 16 * place_of(i, slot) + 8 * kind
+        value = stacked(part[at : at + 8, :])
         for e, copy in coming[i].get(node, []):
             copy.wait_recv()
             value = value + into[e].astype(F32)
         return value
 
     def scatter_send(i, e):
-        at, out, into, rows = rings[i][1], rings[i][3], rings[i][4], rings[i][7]
+        at, out, into, rows = rings[i][1], rings[i][3], rings[i][4], rings[i][6]
         if e >= len(rows):
             return
         node, parent, cross, jump = rows[e]
@@ -287,40 +294,43 @@
             for i in (0, 1):
                 scatter_send(i, e)
 
-    leaves = 8 if nz == 8 or ny == 8 else 1
-    for i in (0, 1):
-        terms(i)
-        for e in range(leaves):
-            scatter_send(i, e)
-    w_par_q = jnp.transpose(w_par).astype(BF16)
-    w_own_q = jnp.concatenate([jnp.transpose(w_own), jnp.transpose(w_g)], axis=1).astype(BF16)
+    leaves = LEAVES if nz == 8 or ny == 8 else 1
+    scatter_sends(0, leaves)
+    settled = len(sent)
+    def in_bank_order(of_h, of_g):
+        cut_h, cut_g = 16 * early[0], 16 * early[1]
+        parts = [of_h[0:cut_h]] * (cut_h > 0) + [of_g[0:cut_g]] * (cut_g > 0)
+        return jnp.transpose(jnp.concatenate(parts + [of_h[cut_h:], of_g[cut_g:]], axis=0))
+
+    w_q = jnp.concatenate(
+        [in_bank_order(w_own, w_g), in_bank_order(w_par, jnp.zeros((rows_g, rows_q), F32))], axis=0
+    ).astype(BF16)
     for h in (0, 1):
         cols = slice(h * wh, (h + 1) * wh)
-        qs[:, cols] = (jnp.dot(w_par_q, bank[0:rows_h, cols], preferred_element_type=F32) * SCALE).astype(BF16)
+        both = jnp.dot(w_q, bank[:, cols], preferred_element_type=F32) * SCALE
+        qf[:, cols] = both[0:rows_q]
+        qs[:, cols] = both[rows_q:].astype(BF16)
     qg_send = send(qs, qr, core_s.at[3], core_r.at[3], other_core)
-    sent.append(qg_send)
-    scatter_sends(leaves, 10)
-    for h in (0, 1):
-        cols = slice(h * wh, (h + 1) * wh)
-        qf[:, cols] = jnp.dot(w_own_q, bank[:, cols], preferred_element_type=F32) * SCALE
-    scatter_sends(10, 13)
+    scatter_sends(leaves, max(leaves, 10))
+    for i in (0, 1):
+        for copy in arrive[i].values():
+            copy.wait_send()
+    for copy in sent[:settled]:
+        copy.wait_send()
+    scatter_sends(max(leaves, 10), 13)
     qg_send.wait_recv()
     qg_ref[...] = qf[...] + qr[...].astype(F32)
     scatter_sends(13, 15)
     total = summed(0, (0, 0)) + summed(1, (0, 0))
     pg_ref[:, 0:wh] = total[0:8]
     pg_ref[:, wh:width] = total[8:16]
-    for i in (0, 1):
-        for copy in arrive[i].values():
-            copy.wait_send()
-    for copy in sent:
+    for copy in sent[settled:] + [qg_send]:
         copy.wait_send()
 
 
-def hand_over(*refs):
-    count = len(refs) // 2
-    sem = refs[-1]
-    copies = [pltpu.make_async_copy(refs[i], refs[count + i], sem.at[i]) for i in range(count)]
+def hand_over(qg_in, pg_in, loss_in, qg, pg, loss, sem):
+    pairs = ((qg_in, qg), (pg_in, pg), (loss_in, loss))
+    copies = [pltpu.make_async_copy(src, dst, sem.at[i]) for i, (src, dst) in enumerate(pairs)]
     for copy in copies:
         copy.start()
     for copy in copies:
@@ -349,15 +359,14 @@
         pltpu.VMEM((nz, 2, 16, wh), BF16),
         pltpu.VMEM((ny, 2, 16, wh), BF16),
         pltpu.VMEM((16 * (nz + ny), width), BF16),
-        pltpu.VMEM((16 * nz, 2 * rows_q), F32),
-        pltpu.VMEM((16 * ny, rows_q), F32),
+        pltpu.VMEM((width, 2 * rows_q), BF16),
+        pltpu.VMEM((16 * (nz + ny), 2 * rows_q), F32),
         pltpu.VMEM((16 * nz, 2 * rows_q), F32),
         pltpu.VMEM((2, 8, rows_q), I32),
         pltpu.VMEM((8, rows_q), I32),
         pltpu.VMEM((8, rows_q), F32),
         pltpu.VMEM((8, rows_q), F32),
-        pltpu.VMEM((16 * nz, width), F32),
-        pltpu.VMEM((16 * ny, width), F32),
+        pltpu.VMEM((16 * (nz + ny), width), F32),
         pltpu.VMEM((2 * nz - 1, 16, wh), BF16),
         pltpu.VMEM((2 * nz - 1, 16, wh), BF16),
         pltpu.VMEM((2 * ny - 1, 16, wh), BF16),

time: 51.2 us -> 47.6 us (0.930)
  Pallas kernels: 50.5 us -> 46.7 us
    pallas_call x1, Pallas kernels: 49.2 us -> 45.4 us  [body(): pl.pallas_call(functools.partial(kernel, nblk, nshard), out_shape=(pltpu....]
where the time goes in v5:
time: 47.6 us; the launch traced here: 47.3 us
  Pallas kernels  46.7 us (98%)
  between operations  0.64 us (1%)
    pallas_call x1, Pallas kernels, body(): pl.pallas_call(functools.partial(kernel, nblk, nshard), out_shape=(pltpu....  45.4 us
    pallas_call x1, Pallas kernels, body(): pl.pallas_call(hand_over, out_shape=tuple((jax.ShapeDtypeStruct(a.shape,...  1.28 us

profile of v5, /device:TPU:1, one launch (start us, length us, event | category | flops | bytes accessed | tf_op | source)
XLA Modules:
  0.0 47.3 jit_solution(8466888101177864117)
XLA Ops:
  0.6 45.4 %shard_map.76 = (f32[128,3584]{1,0:T(8,128)S(1)}, f32[8,3584]{1,0:T(8,128)S(1)}, f32[1,128]{1,0:T(1,128)S(1)}) custom-call(f32[128,3584]{1,0:T(8,128)} %q_hbm.1, f32[8,3584]{1,0:T(8,128)} %p_hbm.1, s32[1,128]{1,0:T(1,128)} %bitcast.6, s32[7,128]{1,0:T(8,128)} %bitcast.4, s32[7,128]{1,0:T(8,128)} %bitcast.5), custom_call_target="tpu_custom_call" | custom-call | tf_op jit(solution)/shard_map/pallas_call | solution.py:382
  46.1 1.3 %shard_map.77 = (f32[128,3584]{1,0:T(8,128)}, f32[8,3584]{1,0:T(8,128)}, f32[1,128]{1,0:T(1,128)}) custom-call(f32[128,3584]{1,0:T(8,128)S(1)} %get-tuple-element.9.qg_in, f32[8,3584]{1,0:T(8,128)S(1)} %get-tuple-element.10.pg_in, f32[1,128]{1,0:T(1,128)S(1)} %get-tuple-element.11.loss_in), custom_call_target="tpu_custom_call" | custom-call | tf_op jit(solution)/shard_map/pallas_call | solution.py:396

commit v6 on v5

--- a/solution.py
+++ b/solution.py
@@ -108,6 +108,9 @@
     sent = []
     p_copy = pltpu.make_async_copy(p_hbm, pf, local_sem.at[0])
     p_copy.start()
+    barrier = pltpu.get_barrier_semaphore()
+    for to in partners.values():
+        pl.semaphore_signal(barrier, inc=1, device_id=to, device_id_type=MESH)
     q_copy = pltpu.make_async_copy(q_hbm, qf, local_sem.at[1])
     q_copy.start()
     index_copies = [
@@ -116,9 +119,6 @@
     ]
     for copy in index_copies:
         copy.start()
-    barrier = pltpu.get_barrier_semaphore()
-    for to in partners.values():
-        pl.semaphore_signal(barrier, inc=1, device_id=to, device_id_type=MESH)
     p_copy.wait()
     mine = stacked(pf[...]).astype(BF16)
     hbuf[0, 0] = mine
@@ -157,7 +157,6 @@
     q_send = send(
         q2.at[pl.ds(0, rows_q)], q2.at[pl.ds(rows_q, rows_q)], core_s.at[0], core_r.at[0], other_core
     )
-    q2t[:, 0:rows_q] = jnp.transpose(q2[0:rows_q, :])
     shift_z, shift_y = max(nz // 2 - 2, 0), max(ny // 2 - 2, 0)
     negs = owner_ref.shape[0]
     for copy in index_copies:
@@ -180,7 +179,6 @@
             named = named | (row_ids == code[k : k + 1, :])
         return jnp.where(named, jnp.float32(0.0), jnp.float32(NONE))
 
-    bias[:, 0:rows_q] = bias_of(codes[0, 0:negs, :])
     p = pos_ref[...]
     g_column = (((p >> 4) - y + (ny + shift_y)) & (ny - 1)) * 16 + (((p >> 3) & 1) ^ xl) * 8 + (p & 7)
     hit = lax.broadcasted_iota(I32, (rows_g, rows_q), 0) == g_column
@@ -211,16 +209,20 @@
 
     gather_sends(first, 15)
     q_send.wait_recv()
+    q2t[:, 0:rows_q] = jnp.transpose(q2[0:rows_q, :])
     q2t[:, rows_q : 2 * rows_q] = jnp.transpose(q2[rows_q : 2 * rows_q, :])
     for i in (0, 1):
         for at in range(early[i]):
             assemble(i, (at - shifts[i]) % rings[i][0])
     scores(0, first_late)
     code_send.wait_recv()
+    bias[:, 0:rows_q] = bias_of(codes[0, 0:negs, :])
     bias[:, rows_q : 2 * rows_q] = bias_of(codes_in[...])
-    for i in (0, 1):
-        for at in range(early[i], rings[i][0]):
-            assemble(i, (at - shifts[i]) % rings[i][0])
+    late = [(at - shifts[i]) % ring[0] for i, ring in enumerate(rings) for at in range(early[i], ring[0])]
+    for slot in sorted(set(late), key=lambda slot: (1, 2, 5, 4, 3, 0, 6, 7).index(slot)):
+        for i in (0, 1):
+            if slot < rings[i][0] and (slot + shifts[i]) % rings[i][0] >= early[i]:
+                assemble(i, slot)
     scores(first_late, rows_h + rows_g)
 
     def ring_rows(ref, i, cols):
@@ -305,22 +307,28 @@
     w_q = jnp.concatenate(
         [in_bank_order(w_own, w_g), in_bank_order(w_par, jnp.zeros((rows_g, rows_q), F32))], axis=0
     ).astype(BF16)
-    for h in (0, 1):
+
+    def query_terms(h):
         cols = slice(h * wh, (h + 1) * wh)
         both = jnp.dot(w_q, bank[:, cols], preferred_element_type=F32) * SCALE
         qf[:, cols] = both[0:rows_q]
         qs[:, cols] = both[rows_q:].astype(BF16)
+
+    scatter_sends(leaves, 9)
+    query_terms(0)
+    scatter_sends(max(leaves, 9), 10)
+    query_terms(1)
     qg_send = send(qs, qr, core_s.at[3], core_r.at[3], other_core)
-    scatter_sends(leaves, max(leaves, 10))
+    scatter_sends(max(leaves, 10), 12)
     for i in (0, 1):
         for copy in arrive[i].values():
             copy.wait_send()
     for copy in sent[:settled]:
         copy.wait_send()
-    scatter_sends(max(leaves, 10), 13)
+    scatter_sends(max(leaves, 12), 14)
     qg_send.wait_recv()
     qg_ref[...] = qf[...] + qr[...].astype(F32)
-    scatter_sends(13, 15)
+    scatter_sends(14, 15)
     total = summed(0, (0, 0)) + summed(1, (0, 0))
     pg_ref[:, 0:wh] = total[0:8]
     pg_ref[:, wh:width] = total[8:16]

time: 47.6 us -> 47.6 us (level)
  no operation moved by 1% of the time
where the time goes in v6:
time: 47.6 us; the launch traced here: 47.4 us
  Pallas kernels  46.8 us (98%)
  between operations  0.64 us (1%)
    pallas_call x1, Pallas kernels, body(): pl.pallas_call(functools.partial(kernel, nblk, nshard), out_shape=(pltpu....  45.5 us
    pallas_call x1, Pallas kernels, body(): pl.pallas_call(hand_over, out_shape=tuple((jax.ShapeDtypeStruct(a.shape,...  1.28 us

profile of v6, /device:TPU:1, one launch (start us, length us, event | category | flops | bytes accessed | tf_op | source)
XLA Modules:
  0.0 47.4 jit_solution(12165272079516494459)
XLA Ops:
  0.6 45.5 %shard_map.76 = (f32[128,3584]{1,0:T(8,128)S(1)}, f32[8,3584]{1,0:T(8,128)S(1)}, f32[1,128]{1,0:T(1,128)S(1)}) custom-call(f32[128,3584]{1,0:T(8,128)} %q_hbm.1, f32[8,3584]{1,0:T(8,128)} %p_hbm.1, s32[1,128]{1,0:T(1,128)} %bitcast.6, s32[7,128]{1,0:T(8,128)} %bitcast.4, s32[7,128]{1,0:T(8,128)} %bitcast.5), custom_call_target="tpu_custom_call" | custom-call | tf_op jit(solution)/shard_map/pallas_call | solution.py:390
  46.1 1.3 %shard_map.77 = (f32[128,3584]{1,0:T(8,128)}, f32[8,3584]{1,0:T(8,128)}, f32[1,128]{1,0:T(1,128)}) custom-call(f32[128,3584]{1,0:T(8,128)S(1)} %get-tuple-element.9.qg_in, f32[8,3584]{1,0:T(8,128)S(1)} %get-tuple-element.10.pg_in, f32[1,128]{1,0:T(1,128)S(1)} %get-tuple-element.11.loss_in), custom_call_target="tpu_custom_call" | custom-call | tf_op jit(solution)/shard_map/pallas_call | solution.py:404

commit v7 on v5

--- a/solution.py
+++ b/solution.py
@@ -157,7 +157,6 @@
     q_send = send(
         q2.at[pl.ds(0, rows_q)], q2.at[pl.ds(rows_q, rows_q)], core_s.at[0], core_r.at[0], other_core
     )
-    q2t[:, 0:rows_q] = jnp.transpose(q2[0:rows_q, :])
     shift_z, shift_y = max(nz // 2 - 2, 0), max(ny // 2 - 2, 0)
     negs = owner_ref.shape[0]
     for copy in index_copies:
@@ -180,7 +179,6 @@
             named = named | (row_ids == code[k : k + 1, :])
         return jnp.where(named, jnp.float32(0.0), jnp.float32(NONE))
 
-    bias[:, 0:rows_q] = bias_of(codes[0, 0:negs, :])
     p = pos_ref[...]
     g_column = (((p >> 4) - y + (ny + shift_y)) & (ny - 1)) * 16 + (((p >> 3) & 1) ^ xl) * 8 + (p & 7)
     hit = lax.broadcasted_iota(I32, (rows_g, rows_q), 0) == g_column
@@ -211,12 +209,14 @@
 
     gather_sends(first, 15)
     q_send.wait_recv()
+    q2t[:, 0:rows_q] = jnp.transpose(q2[0:rows_q, :])
     q2t[:, rows_q : 2 * rows_q] = jnp.transpose(q2[rows_q : 2 * rows_q, :])
     for i in (0, 1):
         for at in range(early[i]):
             assemble(i, (at - shifts[i]) % rings[i][0])
     scores(0, first_late)
     code_send.wait_recv()
+    bias[:, 0:rows_q] = bias_of(codes[0, 0:negs, :])
     bias[:, rows_q : 2 * rows_q] = bias_of(codes_in[...])
     for i in (0, 1):
         for at in range(early[i], rings[i][0]):
@@ -297,6 +297,7 @@
     leaves = LEAVES if nz == 8 or ny == 8 else 1
     scatter_sends(0, leaves)
     settled = len(sent)
+    scatter_sends(leaves, max(leaves, 10))
     def in_bank_order(of_h, of_g):
         cut_h, cut_g = 16 * early[0], 16 * early[1]
         parts = [of_h[0:cut_h]] * (cut_h > 0) + [of_g[0:cut_g]] * (cut_g > 0)
@@ -311,7 +312,6 @@
         qf[:, cols] = both[0:rows_q]
         qs[:, cols] = both[rows_q:].astype(BF16)
     qg_send = send(qs, qr, core_s.at[3], core_r.at[3], other_core)
-    scatter_sends(leaves, max(leaves, 10))
     for i in (0, 1):
         for copy in arrive[i].values():
             copy.wait_send()

time: 47.6 us -> 47.6 us (level)
  no operation moved by 1% of the time
where the time goes in v7:
time: 47.6 us; the launch traced here: 47.3 us
  Pallas kernels  46.7 us (98%)
  between operations  0.64 us (1%)
    pallas_call x1, Pallas kernels, body(): pl.pallas_call(functools.partial(kernel, nblk, nshard), out_shape=(pltpu....  45.4 us
    pallas_call x1, Pallas kernels, body(): pl.pallas_call(hand_over, out_shape=tuple((jax.ShapeDtypeStruct(a.shape,...  1.28 us

profile of v7, /device:TPU:1, one launch (start us, length us, event | category | flops | bytes accessed | tf_op | source)
XLA Modules:
  0.0 47.3 jit_solution(8704105140204872819)
XLA Ops:
  0.6 45.4 %shard_map.76 = (f32[128,3584]{1,0:T(8,128)S(1)}, f32[8,3584]{1,0:T(8,128)S(1)}, f32[1,128]{1,0:T(1,128)S(1)}) custom-call(f32[128,3584]{1,0:T(8,128)} %q_hbm.1, f32[8,3584]{1,0:T(8,128)} %p_hbm.1, s32[1,128]{1,0:T(1,128)} %bitcast.6, s32[7,128]{1,0:T(8,128)} %bitcast.4, s32[7,128]{1,0:T(8,128)} %bitcast.5), custom_call_target="tpu_custom_call" | custom-call | tf_op jit(solution)/shard_map/pallas_call | solution.py:382
  46.0 1.3 %shard_map.77 = (f32[128,3584]{1,0:T(8,128)}, f32[8,3584]{1,0:T(8,128)}, f32[1,128]{1,0:T(1,128)}) custom-call(f32[128,3584]{1,0:T(8,128)S(1)} %get-tuple-element.9.qg_in, f32[8,3584]{1,0:T(8,128)S(1)} %get-tuple-element.10.pg_in, f32[1,128]{1,0:T(1,128)S(1)} %get-tuple-element.11.loss_in), custom_call_target="tpu_custom_call" | custom-call | tf_op jit(solution)/shard_map/pallas_call | solution.py:396
